TPU v7x, 256 devices: a whole 4x4x8 slice. The times are simulated.
256 devices in a mesh: space: 64 (over z, x, core), inst: 4 (over y).
Axes of the slice: x: 4, y: 4, z: 8, core: 2. Of those that a mesh axis runs over, the one named last changes fastest.
Arguments:
- basis_rows: bfloat16 [2, 196608, 512], P(None, 'space'), may hold values from -0.75 to 0.75
- reference_state: float32 [2, 196608], P(None, 'space'), may hold values from -3 to 3
- burning: int32 [196608], P('space'), may hold values 0 or 1
- coords_now: float32 [4, 512], P('inst'), may hold values from -1.5 to 1.5
- coords_before: float32 [4, 512], P('inst'), may hold values from -1.5 to 1.5
- diffusivity: float32 [4], P('inst'), may hold values from 0.5 to 2
- advection: float32 [4], P('inst'), may hold values from 0.5 to 1.5
- reaction_rate: float32 [4], P('inst'), may hold values from 0.2 to 1
Outputs:
- jacobian: bfloat16 [4, 2, 196608, 512], P('inst', None, 'space')
- residual: float32 [4, 2, 196608], P('inst', None, 'space')
- update: float32 [4, 512], P('inst')
All inputs are finite; a program needn't handle non-finite values. No bound on the sum of `burning` on one device may be relied on, other than what follows from the above.
Results may differ from a plain program's by a relative error of at most 0.0034.
Values may be sent and summed in bfloat16 or wider, within the bound.
No kernel may reach another device: no remote copies, remote signals or barrier semaphores. Data moves between devices by JAX's collectives and lax.ppermute only.
A program may use at most 128 MiB of HBM per device.

v0:
```python
import functools

import jax
import jax.numpy as jnp
from jax import lax
from jax.experimental import pallas as pl
from jax.experimental.pallas import tpu as pltpu
from jax.sharding import Mesh
from jax.sharding import PartitionSpec as P

PLANE = ("space_0", "space_1")
CORE = "space_2"
SPACE = (*PLANE, CORE)
F32 = jnp.float32
BF16 = jnp.bfloat16

time_step = 0.5
LANE = 128
STEP_CELLS = 512
EXACT = lax.Precision.HIGHEST


def dot_rows(a, b):
    return lax.dot_general(a, b, (((1,), (1,)), ((), ())), preferred_element_type=F32)


def dot_columns(a, b):
    return lax.dot_general(a, b, (((0,), (0,)), ((), ())), preferred_element_type=F32)


def tile_pairs(count):
    return [(i, j) for i in range(count) for j in range(i, count)]


def rows_kernel(
    core_ref, nu_ref, adv_ref, rate_ref, basis_ref, before_ref, after_ref, halo_low_ref, halo_high_ref,
    ref_ref, burn_ref, now_ref, old_ref, jac_ref, res_ref, own_ref, other_ref, acc, right, *, steps, size
):
    step = pl.program_id(0)
    modes = basis_ref.shape[2]
    nu, adv, rate = nu_ref[0], adv_ref[0], rate_ref[0]
    now = now_ref[...].astype(BF16)
    diff = (now_ref[...] - old_ref[...]).astype(BF16)
    now32 = now.astype(F32)
    coords = jnp.concatenate([now, diff, jnp.zeros((6, modes), BF16)], axis=0)
    first, last = step == 0, step == steps - 1
    start = pl.multiple_of(step * size, size)
    lanes = lax.broadcasted_iota(jnp.int32, (1, size), 1)
    edge, state, moved, flux = [], [], [], []
    for v in range(2):
        low = jnp.where(first, halo_low_ref[v : v + 1, :modes], before_ref[v, 15:16, :].astype(F32))
        high = jnp.where(last, halo_high_ref[v : v + 1, :modes], after_ref[v, 0:1, :].astype(F32))
        edge.append((low, high))
        both = dot_rows(coords, basis_ref[v])
        here = ref_ref[v : v + 1, pl.ds(start, size)] + both[0:1]
        below = pl.multiple_of(jnp.maximum(start - LANE, 0), LANE)
        above = pl.multiple_of(jnp.minimum(start + size, (steps - 1) * size), LANE)
        ref_low = ref_ref[v : v + 1, pl.ds(below, LANE)][:, LANE - 1 : LANE]
        ref_high = ref_ref[v : v + 1, pl.ds(above, LANE)][:, 0:1]
        ref_low = jnp.where(first, halo_low_ref[v : v + 1, modes : modes + 1], ref_low)
        ref_high = jnp.where(last, halo_high_ref[v : v + 1, modes : modes + 1], ref_high)
        state_low = ref_low + jnp.sum(low * now32, axis=1, keepdims=True)
        state_high = ref_high + jnp.sum(high * now32, axis=1, keepdims=True)
        left = jnp.where(lanes == 0, state_low, pltpu.roll(here, 1, 1))
        following = jnp.where(lanes == size - 1, state_high, pltpu.roll(here, size - 1, 1))
        flux.append(nu * (left - 2.0 * here + following) - adv * (here - left))
        state.append(here)
        moved.append(both[1:2])
    active = burn_ref[0:1, pl.ds(start, size)].astype(F32)
    tangent = jnp.tanh(state[1])
    a = rate * active * (1.0 + tangent)
    w = a * state[0]
    e = rate * active * state[0] * (1.0 - tangent * tangent)
    res = [moved[0] - time_step * (flux[0] - w), moved[1] - time_step * (flux[1] + w)]
    res_ref[0:1, :] = res[0]
    res_ref[1:2, :] = res[1]
    mid = 1.0 + time_step * (2.0 * nu + adv)
    lower = time_step * (nu + adv)
    upper = time_step * nu
    rows = lax.broadcasted_iota(jnp.int32, (LANE, modes), 0)
    for t in range(size // LANE):
        lo = LANE * t
        a_col = jnp.broadcast_to(time_step * a[:, lo : lo + LANE], (LANE, LANE)).T
        e_col = jnp.broadcast_to(time_step * e[:, lo : lo + LANE], (LANE, LANE)).T
        a_col = jnp.concatenate([a_col] * (modes // LANE), axis=1)
        e_col = jnp.concatenate([e_col] * (modes // LANE), axis=1)
        parts, mids = [], []
        for v in range(2):
            x = basis_ref[v, lo : lo + LANE, :].astype(F32)
            low = edge[v][0] if t == 0 else basis_ref[v, lo - 16 : lo, :].astype(F32)[15:16]
            end = lo + LANE
            high = edge[v][1] if end == size else basis_ref[v, end : end + 16, :].astype(F32)[0:1]
            left = jnp.where(rows == 0, low, pltpu.roll(x, 1, 0))
            following = jnp.where(rows == LANE - 1, high, pltpu.roll(x, LANE - 1, 0))
            parts.append(mid * x - lower * left - upper * following)
            mids.append(x)
        source = a_col * mids[0] + e_col * mids[1]
        jac_ref[0, lo : lo + LANE, :] = (parts[0] + source).astype(BF16)
        jac_ref[1, lo : lo + LANE, :] = (parts[1] - source).astype(BF16)
    j0, j1 = jac_ref[0], jac_ref[1]
    r = jnp.dot(jnp.broadcast_to(res[0].astype(BF16), (8, size)), j0, preferred_element_type=F32)
    r += jnp.dot(jnp.broadcast_to(res[1].astype(BF16), (8, size)), j1, preferred_element_type=F32)
    half = modes // 2
    top = dot_columns(j0[:, :half], j0) + dot_columns(j1[:, :half], j1)
    bottom = dot_columns(j0[:, half:], j0[:, half:]) + dot_columns(j1[:, half:], j1[:, half:])

    @pl.when(first)
    def _():
        acc[0:half, :] = top
        acc[half:, half:] = bottom
        right[...] = r

    @pl.when(jnp.logical_not(first))
    def _():
        acc[0:half, :] += top
        acc[half:, half:] += bottom
        right[...] += r

    def write(target, which):
        pairs = tile_pairs(modes // LANE)
        rows_half = target.shape[0]
        base = which * rows_half
        for t, (i, j) in enumerate(pairs):
            at = LANE * t - base
            if 0 <= at < rows_half:
                target[at : at + LANE, :] = acc[LANE * i : LANE * i + LANE, LANE * j : LANE * j + LANE]
        at = LANE * len(pairs) - base
        if 0 <= at < rows_half:
            target[at:, :] = jnp.zeros((rows_half - at, LANE), F32)
            for i in range(modes // LANE):
                target[at + 8 * i : at + 8 * i + 1, :] = right[0:1, LANE * i : LANE * i + LANE]

    for core in range(2):

        @pl.when(last & (core_ref[0] == core))
        def _():
            write(own_ref, core)
            write(other_ref, 1 - core)


def packed_rows(modes):
    count = modes // LANE
    return -(-(LANE * len(tile_pairs(count)) + 8 * count) // 512) * 512


def rows_and_sums(core, nu, adv, rate, basis, halo_low, halo_high, ref, burn, now, old):
    cells, modes = basis.shape[1:]
    size = STEP_CELLS
    steps = cells // size
    per = size // 16
    smem = pl.BlockSpec(memory_space=pltpu.SMEM)
    half = packed_rows(modes) // 2

    def whole(shape):
        return pl.BlockSpec(shape, lambda i: (0,) * len(shape))

    return pl.pallas_call(
        functools.partial(rows_kernel, steps=steps, size=size),
        grid=(steps,),
        in_specs=[
            smem, smem, smem, smem,
            pl.BlockSpec((2, size, modes), lambda i: (0, i, 0)),
            pl.BlockSpec((2, 16, modes), lambda i: (0, jnp.maximum(i * per - 1, 0), 0)),
            pl.BlockSpec((2, 16, modes), lambda i: (0, jnp.minimum(i * per + per, cells // 16 - 1), 0)),
            whole(halo_low.shape), whole(halo_high.shape), whole(ref.shape), whole(burn.shape),
            whole(now.shape), whole(old.shape),
        ],
        out_specs=[
            pl.BlockSpec((2, size, modes), lambda i: (0, i, 0)),
            pl.BlockSpec((2, size), lambda i: (0, i)),
            whole((half, LANE)),
            whole((half, LANE)),
        ],
        out_shape=[
            jax.ShapeDtypeStruct((2, cells, modes), BF16),
            jax.ShapeDtypeStruct((2, cells), F32),
            jax.ShapeDtypeStruct((half, LANE), F32),
            jax.ShapeDtypeStruct((half, LANE), F32),
        ],
        scratch_shapes=[pltpu.VMEM((modes, modes), F32), pltpu.VMEM((8, modes), F32)],
        compiler_params=pltpu.CompilerParams(vmem_limit_bytes=48 * 2**20),
    )(core, nu, adv, rate, basis, basis, basis, halo_low, halo_high, ref, burn, now, old)


def reciprocal(x):
    y = pltpu.reciprocal(x, approx=True)
    y = y * (2.0 - x * y)
    return y * (2.0 - x * y)


def inverse_block(block):
    width = block.shape[1]
    groups = [block[8 * g : 8 * g + 8] for g in range(width // 8)]
    full = (8, width)
    lanes = lax.broadcasted_iota(jnp.int32, full, 1)
    subs = lax.broadcasted_iota(jnp.int32, full, 0)
    for p in range(len(groups)):
        panel = groups[p]
        base = 8 * p
        cols = [jnp.broadcast_to(panel[:, base + j : base + j + 1], full) for j in range(8)]
        entry = [[jnp.broadcast_to(cols[t][s : s + 1], full) if t >= s else None for t in range(8)] for s in range(8)]
        window = (lanes >= base) & (lanes < base + 8)
        opened = jnp.where(window, jnp.where(lanes == subs + base, 1.0, 0.0), panel)
        rows = [jnp.broadcast_to(opened[s : s + 1], full) for s in range(8)]
        inv = []
        for j in range(8):
            inv.append(reciprocal(entry[j][j]))
            for s in [*range(j + 1, 8), *range(j)]:
                mult = (entry[j][s] if s > j else entry[s][j]) * inv[j]
                for t in range(max(s, j + 1), 8):
                    entry[s][t] = entry[s][t] - mult * entry[j][t]
                rows[s] = rows[s] - mult * rows[j]
        rows = [rows[s] * inv[s] for s in range(8)]
        for g in range(len(groups)):
            if g == p:
                continue
            terms = [jnp.broadcast_to(groups[g][:, base + s : base + s + 1], full) * rows[s] for s in range(8)]
            while len(terms) > 1:
                terms = [a + b for a, b in zip(terms[::2], terms[1::2])]
            groups[g] = jnp.where(window, 0.0, groups[g]) - terms[0]
        whole = rows[0]
        for s in range(1, 8):
            whole = jnp.where(subs == s, rows[s], whole)
        groups[p] = whole
    return jnp.concatenate(groups, axis=0)


def exact_dot(a, b, dims=((1,), (0,))):
    return lax.dot_general(a, b, (dims, ((), ())), precision=EXACT, preferred_element_type=F32)


def solve_kernel(core_ref, own_ref, other_ref, out_ref, packed, work, panel, *, count):
    half = own_ref.shape[0]
    core = core_ref[0]
    packed[pl.ds(pl.multiple_of(core * half, half), half), :] = own_ref[...]
    packed[pl.ds(pl.multiple_of((1 - core) * half, half), half), :] = other_ref[...]
    modes = count * LANE
    pairs = tile_pairs(count)
    for t, (i, j) in enumerate(pairs):
        work[LANE * i : LANE * i + LANE, LANE * j : LANE * j + LANE] = packed[LANE * t : LANE * t + LANE, :]
    for i in range(count):
        at = LANE * len(pairs) + 8 * i
        r = jnp.broadcast_to(packed[at : at + 1, :], (LANE, LANE))
        work[LANE * i : LANE * i + LANE, modes : modes + LANE] = r.T
    for k in range(count):
        lo = LANE * k
        end = lo + LANE
        x = exact_dot(inverse_block(work[lo:end, lo:end]), work[lo:end, end:])
        panel[lo:end, end:] = x
        for i in range(k + 1, count):
            a = LANE * i
            work[a : a + LANE, a:] -= exact_dot(work[lo:end, a : a + LANE], x[:, a - end :], ((0,), (0,)))
    solved = {}
    for k in reversed(range(count)):
        lo = LANE * k
        u = panel[lo : lo + LANE, modes:]
        for i in range(k + 1, count):
            u = u - exact_dot(panel[lo : lo + LANE, LANE * i : LANE * i + LANE], solved[i])
        solved[k] = u
        out_ref[0:1, lo : lo + LANE] = -u.T[0:1]


def solve_update(core, own, other, modes):
    vmem = pl.BlockSpec(memory_space=pltpu.VMEM)
    return pl.pallas_call(
        functools.partial(solve_kernel, count=modes // LANE),
        out_shape=jax.ShapeDtypeStruct((1, modes), F32),
        in_specs=[pl.BlockSpec(memory_space=pltpu.SMEM), vmem, vmem],
        out_specs=vmem,
        scratch_shapes=[
            pltpu.VMEM((2 * own.shape[0], LANE), F32),
            pltpu.VMEM((modes, modes + LANE), F32),
            pltpu.VMEM((modes, modes + LANE), F32),
        ],
        compiler_params=pltpu.CompilerParams(vmem_limit_bytes=48 * 2**20),
    )(core, own, other)


def swapped(shard):
    return lax.ppermute(shard, CORE, [(0, 1), (1, 0)])


def summed_over_plane(shard):
    count = lax.axis_size(PLANE)
    blocks = shard.reshape(count, shard.shape[0] // count, shard.shape[1])
    mine = jnp.sum(lax.all_to_all(blocks, PLANE, 0, 0, tiled=True), axis=0)
    copies = jnp.broadcast_to(mine, blocks.shape)
    return lax.all_to_all(copies, PLANE, 0, 0, tiled=True).reshape(shard.shape)


def edge_message(basis_row, state_value):
    return jnp.concatenate([basis_row.astype(F32), jnp.pad(state_value, ((0, 0), (0, LANE - 1)))], axis=1)


def on_device(
    basis_rows,
    reference_state,
    burning,
    coords_now,
    coords_before,
    diffusivity,
    advection,
    reaction_rate,
):
    modes = basis_rows.shape[2]
    size = lax.axis_size(SPACE)
    core = lax.axis_index(CORE).reshape(1)
    up = [(i, i + 1) for i in range(size - 1)]
    halo_low = lax.ppermute(edge_message(basis_rows[:, -1], reference_state[:, -1:]), SPACE, up)
    halo_high = lax.ppermute(
        edge_message(basis_rows[:, 0], reference_state[:, :1]), SPACE, [(j, i) for i, j in up]
    )
    jacobian, residual, own, other = rows_and_sums(
        core, diffusivity, advection, reaction_rate, basis_rows, halo_low, halo_high,
        reference_state, burning[None], coords_now, coords_before,
    )
    half = summed_over_plane(own + swapped(other))
    update = solve_update(core, half, swapped(half), modes)
    return (jacobian[None], residual[None], update)


def solution(mesh):
    split = Mesh(
        mesh.devices.reshape(8, 4, 2, mesh.shape["inst"]), ("space_0", "space_1", "space_2", "inst")
    )
    placed = (
        P(None, SPACE, None),
        P(None, SPACE),
        P(SPACE),
        P("inst", None),
        P("inst", None),
        P("inst"),
        P("inst"),
        P("inst"),
    )
    return jax.shard_map(
        on_device,
        mesh=split,
        in_specs=placed,
        out_specs=(P("inst", None, SPACE, None), P("inst", None, SPACE), P("inst", None)),
        check_vma=False,
    )
```

profile of v0, /device:TPU:1, one launch (start us, length us, event | category | flops | bytes accessed | tf_op | source)
XLA Modules:
  0.0 108.5 jit_solution(16884818058500712799)
XLA Ops:
  0.6 0.8 slice.14
  1.4 0.7 fusion.3
  2.2 4.5 %collective-permute-start = (f32[2,640]{1,0:T(2,128)S(1)}, f32[2,640]{1,0:T(2,128)S(1)}, u32[]{:S(2)}, u32[]{:S(2)}) collective-permute-start(f32[2,640]{1,0:T(2,128)S(1)} %fusion), channel_id=1, source_target_pairs={{0,4},{4,8},{8,12},{12,16},{16,20},{20,24},{24,28},{28,32},{32,36}... | collective-permute-start | bytes 15368 | tf_op jit(solution)/shard_map/ppermute | solution.py:309
  6.7 0.7 slice_select_fusion
  7.4 1.9 %collective-permute-start.1 = (f32[2,640]{1,0:T(2,128)S(1)}, f32[2,640]{1,0:T(2,128)S(1)}, u32[]{:S(2)}, u32[]{:S(2)}) collective-permute-start(f32[2,640]{1,0:T(2,128)S(1)} %pad_maximum_fusion), channel_id=1, source_target_pairs={{4,0},{8,4},{12,8},{16,12},{20,16},{24,20},{28,24},{32,28},{36,32}... | collective-permute-start | bytes 15368 | tf_op jit(solution)/shard_map/ppermute | solution.py:310
  11.3 0.0 collective-permute-done.halo_low_ref
  11.3 1.0 collective-permute-done.1.halo_high_ref
  12.3 0.0 copy-start
  12.3 0.7 copy-done
  13.1 0.0 copy-start.1
  13.1 0.7 copy-done.1
  13.8 0.0 copy-start.2
  13.8 0.7 copy-done.2
  14.4 0.0 copy-start.3
  14.4 0.7 copy-done.3
  15.1 17.5 %shard_map.103 = (bf16[2,3072,512]{2,1,0:T(8,128)(2,1)}, f32[2,3072]{1,0:T(2,128)}, f32[768,128]{1,0:T(8,128)S(1)}, f32[768,128]{1,0:T(8,128)S(1)}) custom-call(s32[1]{0:T(128)} %bitcast.core_ref, f32[1]{0:T(128)S(6)} %copy.21.nu_ref, f32[1]{0:T(128)S(6)} %copy.22.adv_ref, f32[1]{0:T(128)S(6)} %copy.23.rate_ref, bf16[2,3072,512]{2,1,0:T(8,128)(2,1)} %after_ref.1, ...), custom_call_target="tpu_custom_call" | custom-call | tf_op jit(solution)/shard_map/pallas_call | solution.py:157
  32.6 0.0 collective-permute-start.2
  32.6 1.7 %collective-permute-done.2 = f32[768,128]{1,0:T(8,128)S(1)} collective-permute-done((f32[768,128]{1,0:T(8,128)S(1)}, f32[768,128]{1,0:T(8,128)S(1)}, u32[]{:S(2)}, u32[]{:S(2)}) %collective-permute-start.2) | collective-permute-done | bytes 393248 | tf_op jit(solution)/shard_map/ppermute | solution.py:280
  34.4 0.1 add.5
  34.4 27.3 %all_to_all.10 = f32[32,24,128]{2,1,0:T(8,128)S(1)} all-to-all(f32[32,24,128]{2,1,0:T(8,128)S(1)} %bitcast.19), channel_id=1, replica_groups=mesh['space_0'=8,'space_1'=4,'space_2'=2,'inst'=4] {'space_0','space_1'}, dimensions={0} | all-to-all | bytes 786432 | tf_op jit(solution)/shard_map/all_to_all | solution.py:286
  61.8 17.1 %all_to_all.11 = f32[32,24,128]{2,1,0:T(8,128)S(1)} all-to-all(f32[32,24,128]{2,1,0:T(8,128)S(1)} %broadcast_in_dim.15), channel_id=1, replica_groups=mesh['space_0'=8,'space_1'=4,'space_2'=2,'inst'=4] {'space_0','space_1'}, dimensions={0} | all-to-all | bytes 786432 | tf_op jit(solution)/shard_map/all_to_all | solution.py:288
  78.9 3.4 %collective-permute-start.3 = (f32[768,128]{1,0:T(8,128)S(1)}, f32[768,128]{1,0:T(8,128)S(1)}, u32[]{:S(2)}, u32[]{:S(2)}) collective-permute-start(f32[768,128]{1,0:T(8,128)S(1)} %bitcast.16), channel_id=1, source_target_pairs={{0,4},{4,0},{1,5},{5,1},{2,6},{6,2},{3,7},{7,3},{8,12},{12,8},{9,1... | collective-permute-start | bytes 1179656 | tf_op jit(solution)/shard_map/ppermute | solution.py:280
  82.3 1.3 %collective-permute-done.3.other_ref = f32[768,128]{1,0:T(8,128)S(1)} collective-permute-done((f32[768,128]{1,0:T(8,128)S(1)}, f32[768,128]{1,0:T(8,128)S(1)}, u32[]{:S(2)}, u32[]{:S(2)}) %collective-permute-start.3) | collective-permute-done | bytes 393248 | tf_op jit(solution)/shard_map/ppermute | solution.py:280
  83.6 24.9 %shard_map.104 = f32[1,512]{1,0:T(1,128)} custom-call(s32[1]{0:T(128)} %bitcast.core_ref, f32[768,128]{1,0:T(8,128)S(1)} %bitcast.17, f32[768,128]{1,0:T(8,128)S(1)} %collective-permute-done.3.other_ref), custom_call_target="tpu_custom_call" | custom-call | tf_op jit(solution)/shard_map/pallas_call | solution.py:265
  (6 shorter events, 0.1 us)
Async XLA Ops:
  2.2 9.1 %collective-permute-start = (f32[2,640]{1,0:T(2,128)S(1)}, f32[2,640]{1,0:T(2,128)S(1)}, u32[]{:S(2)}, u32[]{:S(2)}) collective-permute-start(f32[2,640]{1,0:T(2,128)S(1)} %fusion), channel_id=1, source_target_pairs={{0,4},{4,8},{8,12},{12,16},{16,20},{20,24},{24,28},{28,32},{32,36}... | collective-permute-start | bytes 15368 | tf_op jit(solution)/shard_map/ppermute | solution.py:309
  7.4 4.9 %collective-permute-start.1 = (f32[2,640]{1,0:T(2,128)S(1)}, f32[2,640]{1,0:T(2,128)S(1)}, u32[]{:S(2)}, u32[]{:S(2)}) collective-permute-start(f32[2,640]{1,0:T(2,128)S(1)} %pad_maximum_fusion), channel_id=1, source_target_pairs={{4,0},{8,4},{12,8},{16,12},{20,16},{24,20},{28,24},{32,28},{36,32}... | collective-permute-start | bytes 15368 | tf_op jit(solution)/shard_map/ppermute | solution.py:310
  12.3 0.7 copy-start
  13.1 0.7 copy-start.1
  13.8 0.7 copy-start.2
  14.4 0.7 copy-start.3
  32.6 1.7 %collective-permute-start.2 = (f32[768,128]{1,0:T(8,128)S(1)}, f32[768,128]{1,0:T(8,128)S(1)}, u32[]{:S(2)}, u32[]{:S(2)}) collective-permute-start(f32[768,128]{1,0:T(8,128)S(1)} %get-tuple-element.10), channel_id=1, source_target_pairs={{0,4},{4,0},{1,5},{5,1},{2,6},{6,2},{3,7},{7,3},{8,12},{12,8},{9,1... | collective-permute-start | bytes 1179656 | tf_op jit(solution)/shard_map/ppermute | solution.py:280
  78.9 4.7 %collective-permute-start.3 = (f32[768,128]{1,0:T(8,128)S(1)}, f32[768,128]{1,0:T(8,128)S(1)}, u32[]{:S(2)}, u32[]{:S(2)}) collective-permute-start(f32[768,128]{1,0:T(8,128)S(1)} %bitcast.16), channel_id=1, source_target_pairs={{0,4},{4,0},{1,5},{5,1},{2,6},{6,2},{3,7},{7,3},{8,12},{12,8},{9,1... | collective-permute-start | bytes 1179656 | tf_op jit(solution)/shard_map/ppermute | solution.py:280
where the time goes:
time: 109 us
  blocking collectives  44.4 us (41%)
  Pallas kernels  42.4 us (39%)
  starting transfers between devices  9.83 us (9%)
  local copies, waits for them, and re-layouts  4.33 us (4%)
  waiting for transfers between devices  4.12 us (4%)
  between operations  2.64 us (2%)
    all_to_all x1, blocking collectives, summed_over_plane(): mine = jnp.sum(lax.all_to_all(blocks, PLANE, 0, 0, tiled=True), axis=0)  27.3 us
    pallas_call x1, Pallas kernels, solve_update(): pl.pallas_call(functools.partial(solve_kernel, count=modes // LANE), out_...  24.9 us
    pallas_call x1, Pallas kernels, rows_and_sums(): pl.pallas_call(functools.partial(rows_kernel, steps=steps, size=size), gr...  17.5 us
    all_to_all x1, blocking collectives, summed_over_plane(): return lax.all_to_all(copies, PLANE, 0, 0, tiled=True).reshape(shard.shape)  17.1 us
    ppermute x1, starting transfers between devices, on_device(): lax.ppermute(edge_message(basis_rows[:, -1], reference_state[:, -1:]), SP...  4.51 us
    ppermute x2, starting transfers between devices, swapped(): return lax.ppermute(shard, CORE, [(0, 1), (1, 0)])  3.39 us
    ppermute x2, waiting for transfers between devices, swapped(): return lax.ppermute(shard, CORE, [(0, 1), (1, 0)])  3.07 us
    unnamed x8, local copies, waits for them, and re-layouts  2.81 us
  transfers between devices with their start and end apart: 4, of which 3 were waited for; matrix products, arithmetic and copies ran while one was open for 1% of the time, Pallas kernels for 0%

commit v1 on v0

--- a/solution.py
+++ b/solution.py
@@ -32,33 +32,47 @@
     return [(i, j) for i in range(count) for j in range(i, count)]
 
 
-def rows_kernel(
-    core_ref, nu_ref, adv_ref, rate_ref, basis_ref, before_ref, after_ref, halo_low_ref, halo_high_ref,
-    ref_ref, burn_ref, now_ref, old_ref, jac_ref, res_ref, own_ref, other_ref, acc, right, *, steps, size
-):
+def rows_kernel(*refs, steps, size, edges):
+    refs = iter(refs)
+    core_ref, nu_ref, adv_ref, rate_ref, basis_ref, before_ref, after_ref = (next(refs) for _ in range(7))
+    ref_ref, burn_ref, now_ref, old_ref = (next(refs) for _ in range(4))
+    if edges:
+        halo_low_ref, halo_high_ref, sums_ref, right_in_ref, _, _ = (next(refs) for _ in range(6))
+        jac_ref, res_ref, own_ref, other_ref, acc, right, wide = refs
+    else:
+        jac_ref, res_ref, acc, right, wide = refs
     step = pl.program_id(0)
+    first, last = step == 0, step == pl.num_programs(0) - 1
+    chunk = step * (steps - 1) if edges else step + 1
     modes = basis_ref.shape[2]
+    tiles = modes // LANE
     nu, adv, rate = nu_ref[0], adv_ref[0], rate_ref[0]
     now = now_ref[...].astype(BF16)
     diff = (now_ref[...] - old_ref[...]).astype(BF16)
     now32 = now.astype(F32)
     coords = jnp.concatenate([now, diff, jnp.zeros((6, modes), BF16)], axis=0)
-    first, last = step == 0, step == steps - 1
-    start = pl.multiple_of(step * size, size)
+    start = pl.multiple_of(chunk * size, size)
     lanes = lax.broadcasted_iota(jnp.int32, (1, size), 1)
-    edge, state, moved, flux = [], [], [], []
+    state, moved, flux = [], [], []
     for v in range(2):
-        low = jnp.where(first, halo_low_ref[v : v + 1, :modes], before_ref[v, 15:16, :].astype(F32))
-        high = jnp.where(last, halo_high_ref[v : v + 1, :modes], after_ref[v, 0:1, :].astype(F32))
-        edge.append((low, high))
-        both = dot_rows(coords, basis_ref[v])
-        here = ref_ref[v : v + 1, pl.ds(start, size)] + both[0:1]
+        low = before_ref[v, 15:16, :].astype(F32)
+        high = after_ref[v, 0:1, :].astype(F32)
         below = pl.multiple_of(jnp.maximum(start - LANE, 0), LANE)
         above = pl.multiple_of(jnp.minimum(start + size, (steps - 1) * size), LANE)
         ref_low = ref_ref[v : v + 1, pl.ds(below, LANE)][:, LANE - 1 : LANE]
         ref_high = ref_ref[v : v + 1, pl.ds(above, LANE)][:, 0:1]
-        ref_low = jnp.where(first, halo_low_ref[v : v + 1, modes : modes + 1], ref_low)
-        ref_high = jnp.where(last, halo_high_ref[v : v + 1, modes : modes + 1], ref_high)
+        if edges:
+            low = jnp.where(first, halo_low_ref[v : v + 1, :modes], low)
+            high = jnp.where(last, halo_high_ref[v : v + 1, :modes], high)
+            ref_low = jnp.where(first, halo_low_ref[v : v + 1, modes : modes + 1], ref_low)
+            ref_high = jnp.where(last, halo_high_ref[v : v + 1, modes : modes + 1], ref_high)
+        for m in range(tiles):
+            cols = slice(LANE * m, LANE * m + LANE)
+            wide[v * tiles + m, 8 : 8 + size, :] = basis_ref[v, :, cols].astype(F32)
+            wide[v * tiles + m, 7:8, :] = low[:, cols]
+            wide[v * tiles + m, 8 + size : 9 + size, :] = high[:, cols]
+        both = dot_rows(coords, basis_ref[v])
+        here = ref_ref[v : v + 1, pl.ds(start, size)] + both[0:1]
         state_low = ref_low + jnp.sum(low * now32, axis=1, keepdims=True)
         state_high = ref_high + jnp.sum(high * now32, axis=1, keepdims=True)
         left = jnp.where(lanes == 0, state_low, pltpu.roll(here, 1, 1))
@@ -77,26 +91,24 @@
     mid = 1.0 + time_step * (2.0 * nu + adv)
     lower = time_step * (nu + adv)
     upper = time_step * nu
-    rows = lax.broadcasted_iota(jnp.int32, (LANE, modes), 0)
+
+    def sides(k, lo):
+        return lower * wide[k, 7 + lo : 7 + lo + LANE, :] + upper * wide[k, 9 + lo : 9 + lo + LANE, :]
+
     for t in range(size // LANE):
         lo = LANE * t
         a_col = jnp.broadcast_to(time_step * a[:, lo : lo + LANE], (LANE, LANE)).T
         e_col = jnp.broadcast_to(time_step * e[:, lo : lo + LANE], (LANE, LANE)).T
-        a_col = jnp.concatenate([a_col] * (modes // LANE), axis=1)
-        e_col = jnp.concatenate([e_col] * (modes // LANE), axis=1)
-        parts, mids = [], []
-        for v in range(2):
-            x = basis_ref[v, lo : lo + LANE, :].astype(F32)
-            low = edge[v][0] if t == 0 else basis_ref[v, lo - 16 : lo, :].astype(F32)[15:16]
-            end = lo + LANE
-            high = edge[v][1] if end == size else basis_ref[v, end : end + 16, :].astype(F32)[0:1]
-            left = jnp.where(rows == 0, low, pltpu.roll(x, 1, 0))
-            following = jnp.where(rows == LANE - 1, high, pltpu.roll(x, LANE - 1, 0))
-            parts.append(mid * x - lower * left - upper * following)
-            mids.append(x)
-        source = a_col * mids[0] + e_col * mids[1]
-        jac_ref[0, lo : lo + LANE, :] = (parts[0] + source).astype(BF16)
-        jac_ref[1, lo : lo + LANE, :] = (parts[1] - source).astype(BF16)
+        fuel_own = mid + a_col
+        heat_own = mid - e_col
+        for m in range(tiles):
+            cols = slice(LANE * m, LANE * m + LANE)
+            p = wide[m, 8 + lo : 8 + lo + LANE, :]
+            q = wide[tiles + m, 8 + lo : 8 + lo + LANE, :]
+            fuel = fuel_own * p + e_col * q - sides(m, lo)
+            heat = heat_own * q - a_col * p - sides(tiles + m, lo)
+            jac_ref[0, lo : lo + LANE, cols] = fuel.astype(BF16)
+            jac_ref[1, lo : lo + LANE, cols] = heat.astype(BF16)
     j0, j1 = jac_ref[0], jac_ref[1]
     r = jnp.dot(jnp.broadcast_to(res[0].astype(BF16), (8, size)), j0, preferred_element_type=F32)
     r += jnp.dot(jnp.broadcast_to(res[1].astype(BF16), (8, size)), j1, preferred_element_type=F32)
@@ -106,15 +118,23 @@
 
     @pl.when(first)
     def _():
-        acc[0:half, :] = top
-        acc[half:, half:] = bottom
-        right[...] = r
+        if edges:
+            acc[0:half, :] = sums_ref[0:half, :] + top
+            acc[half:, half:] = sums_ref[half:, half:] + bottom
+            right[...] = right_in_ref[...] + r
+        else:
+            acc[0:half, :] = top
+            acc[half:, half:] = bottom
+            right[...] = r
 
     @pl.when(jnp.logical_not(first))
     def _():
         acc[0:half, :] += top
         acc[half:, half:] += bottom
         right[...] += r
+
+    if not edges:
+        return
 
     def write(target, which):
         pairs = tile_pairs(modes // LANE)
@@ -143,49 +163,71 @@
     return -(-(LANE * len(tile_pairs(count)) + 8 * count) // 512) * 512
 
 
-def rows_and_sums(core, nu, adv, rate, basis, halo_low, halo_high, ref, burn, now, old):
+def rows_call(core, nu, adv, rate, basis, ref, burn, now, old, edge_args=None):
     cells, modes = basis.shape[1:]
     size = STEP_CELLS
     steps = cells // size
     per = size // 16
+    edges = edge_args is not None
     smem = pl.BlockSpec(memory_space=pltpu.SMEM)
     half = packed_rows(modes) // 2
 
+    def chunk(i):
+        return i * (steps - 1) if edges else i + 1
+
     def whole(shape):
         return pl.BlockSpec(shape, lambda i: (0,) * len(shape))
 
+    in_specs = [
+        smem, smem, smem, smem,
+        pl.BlockSpec((2, size, modes), lambda i: (0, chunk(i), 0)),
+        pl.BlockSpec((2, 16, modes), lambda i: (0, jnp.maximum(chunk(i) * per - 1, 0), 0)),
+        pl.BlockSpec((2, 16, modes), lambda i: (0, jnp.minimum(chunk(i) * per + per, cells // 16 - 1), 0)),
+        whole(ref.shape), whole(burn.shape), whole(now.shape), whole(old.shape),
+    ]
+    out_specs = [
+        pl.BlockSpec((2, size, modes), lambda i: (0, chunk(i), 0)),
+        pl.BlockSpec((2, size), lambda i: (0, chunk(i))),
+    ]
+    out_shape = [
+        jax.ShapeDtypeStruct((2, cells, modes), BF16),
+        jax.ShapeDtypeStruct((2, cells), F32),
+    ]
+    sums_shape = [jax.ShapeDtypeStruct((modes, modes), F32), jax.ShapeDtypeStruct((8, modes), F32)]
+    scratch = [pltpu.VMEM((2 * (modes // LANE), size + 16, LANE), F32)]
+    args = [core, nu, adv, rate, basis, basis, basis, ref, burn, now, old]
+    aliases = {}
+    if edges:
+        anywhere = pl.BlockSpec(memory_space=pl.ANY)
+        args += edge_args
+        in_specs += [whole(a.shape) for a in edge_args[:4]] + [anywhere, anywhere]
+        out_specs += [whole((half, LANE))] * 2
+        out_shape += [jax.ShapeDtypeStruct((half, LANE), F32)] * 2
+        scratch = [pltpu.VMEM(s.shape, s.dtype) for s in sums_shape] + scratch
+        aliases = {len(args) - 2: 0, len(args) - 1: 1}
+    else:
+        out_specs += [whole(s.shape) for s in sums_shape]
+        out_shape += sums_shape
     return pl.pallas_call(
-        functools.partial(rows_kernel, steps=steps, size=size),
-        grid=(steps,),
-        in_specs=[
-            smem, smem, smem, smem,
-            pl.BlockSpec((2, size, modes), lambda i: (0, i, 0)),
-            pl.BlockSpec((2, 16, modes), lambda i: (0, jnp.maximum(i * per - 1, 0), 0)),
-            pl.BlockSpec((2, 16, modes), lambda i: (0, jnp.minimum(i * per + per, cells // 16 - 1), 0)),
-            whole(halo_low.shape), whole(halo_high.shape), whole(ref.shape), whole(burn.shape),
-            whole(now.shape), whole(old.shape),
-        ],
-        out_specs=[
-            pl.BlockSpec((2, size, modes), lambda i: (0, i, 0)),
-            pl.BlockSpec((2, size), lambda i: (0, i)),
-            whole((half, LANE)),
-            whole((half, LANE)),
-        ],
-        out_shape=[
-            jax.ShapeDtypeStruct((2, cells, modes), BF16),
-            jax.ShapeDtypeStruct((2, cells), F32),
-            jax.ShapeDtypeStruct((half, LANE), F32),
-            jax.ShapeDtypeStruct((half, LANE), F32),
-        ],
-        scratch_shapes=[pltpu.VMEM((modes, modes), F32), pltpu.VMEM((8, modes), F32)],
+        functools.partial(rows_kernel, steps=steps, size=size, edges=edges),
+        grid=(2 if edges else steps - 2,),
+        in_specs=in_specs,
+        out_specs=out_specs,
+        out_shape=out_shape,
+        scratch_shapes=scratch,
+        input_output_aliases=aliases,
         compiler_params=pltpu.CompilerParams(vmem_limit_bytes=48 * 2**20),
-    )(core, nu, adv, rate, basis, basis, basis, halo_low, halo_high, ref, burn, now, old)
+    )(*args)
+
+
+def rows_and_sums(core, nu, adv, rate, basis, halo_low, halo_high, ref, burn, now, old):
+    common = (core, nu, adv, rate, basis, ref, burn, now, old)
+    jacobian, residual, sums, right = rows_call(*common)
+    return rows_call(*common, [halo_low, halo_high, sums, right, jacobian, residual])
 
 
 def reciprocal(x):
-    y = pltpu.reciprocal(x, approx=True)
-    y = y * (2.0 - x * y)
-    return y * (2.0 - x * y)
+    return pltpu.reciprocal(x, approx=True)
 
 
 def inverse_block(block):
@@ -240,7 +282,7 @@
         work[LANE * i : LANE * i + LANE, LANE * j : LANE * j + LANE] = packed[LANE * t : LANE * t + LANE, :]
     for i in range(count):
         at = LANE * len(pairs) + 8 * i
-        r = jnp.broadcast_to(packed[at : at + 1, :], (LANE, LANE))
+        r = jnp.broadcast_to(packed[at : at + 1, :] + packed[at + 1 : at + 2, :], (LANE, LANE))
         work[LANE * i : LANE * i + LANE, modes : modes + LANE] = r.T
     for k in range(count):
         lo = LANE * k
@@ -280,10 +322,13 @@
     return lax.ppermute(shard, CORE, [(0, 1), (1, 0)])
 
 
-def summed_over_plane(shard):
+def summed_over_plane(shard, low_rows):
     count = lax.axis_size(PLANE)
-    blocks = shard.reshape(count, shard.shape[0] // count, shard.shape[1])
-    mine = jnp.sum(lax.all_to_all(blocks, PLANE, 0, 0, tiled=True), axis=0)
+    rounded = shard.astype(BF16)
+    left_over = jnp.roll(shard - rounded.astype(F32), 1, axis=0).astype(BF16)
+    sent = jnp.where(low_rows, left_over, rounded)
+    blocks = sent.reshape(count, shard.shape[0] // count, shard.shape[1])
+    mine = jnp.sum(lax.all_to_all(blocks, PLANE, 0, 0, tiled=True).astype(F32), axis=0)
     copies = jnp.broadcast_to(mine, blocks.shape)
     return lax.all_to_all(copies, PLANE, 0, 0, tiled=True).reshape(shard.shape)
 
@@ -314,7 +359,10 @@
         core, diffusivity, advection, reaction_rate, basis_rows, halo_low, halo_high,
         reference_state, burning[None], coords_now, coords_before,
     )
-    half = summed_over_plane(own + swapped(other))
+    row = core * own.shape[0] + jnp.arange(own.shape[0], dtype=jnp.int32)
+    begin = LANE * len(tile_pairs(modes // LANE))
+    low_rows = ((row >= begin) & (row % 8 == 1))[:, None]
+    half = summed_over_plane(own + swapped(other), low_rows)
     update = solve_update(core, half, swapped(half), modes)
     return (jacobian[None], residual[None], update)
 

time: 109 us -> 102 us (0.936)
  blocking collectives: 44.4 us -> 39.3 us
  Pallas kernels: 42.4 us -> 40.9 us
    all_to_all x1, blocking collectives: 27.3 us -> 22.5 us  [summed_over_plane(): lax.all_to_all(blocks, PLANE, 0, 0, tiled=True).astype(F32)]
    pallas_call x1, Pallas kernels: 24.9 us -> 22.4 us  [solve_update(): pl.pallas_call(functools.partial(solve_kernel, count=modes // LANE), out_...]
    pallas_call x1 -> x2, Pallas kernels: 17.5 us -> 18.5 us  [rows_call(): pl.pallas_call(functools.partial(rows_kernel, steps=steps, size=size, edg...]
  transfers between devices with their start and end apart: 4 -> 4, of which waited for: 3 -> 2; matrix products, arithmetic and copies ran while one was open for 1% -> 1% of each run, Pallas kernels for 0% -> 11%
where the time goes in v1:
time: 102 us; the launch traced here: 101 us
  Pallas kernels  40.9 us (40%)
  blocking collectives  39.3 us (39%)
  starting transfers between devices  9.86 us (10%)
  local copies, waits for them, and re-layouts  4.34 us (4%)
  waiting for transfers between devices  3.06 us (3%)
  between operations  2.66 us (3%)
    all_to_all x1, blocking collectives, summed_over_plane(): lax.all_to_all(blocks, PLANE, 0, 0, tiled=True).astype(F32)  22.5 us
    pallas_call x1, Pallas kernels, solve_update(): pl.pallas_call(functools.partial(solve_kernel, count=modes // LANE), out_...  22.4 us
    pallas_call x2, Pallas kernels, rows_call(): pl.pallas_call(functools.partial(rows_kernel, steps=steps, size=size, edg...  18.5 us
    all_to_all x1, blocking collectives, summed_over_plane(): return lax.all_to_all(copies, PLANE, 0, 0, tiled=True).reshape(shard.shape)  16.8 us
    ppermute x1, starting transfers between devices, on_device(): lax.ppermute(edge_message(basis_rows[:, -1], reference_state[:, -1:]), SP...  4.5 us
    ppermute x2, starting transfers between devices, swapped(): return lax.ppermute(shard, CORE, [(0, 1), (1, 0)])  3.43 us
    ppermute x2, waiting for transfers between devices, swapped(): return lax.ppermute(shard, CORE, [(0, 1), (1, 0)])  3.06 us
    unnamed x8, local copies, waits for them, and re-layouts  2.8 us
  transfers between devices with their start and end apart: 4, of which 2 were waited for; matrix products, arithmetic and copies ran while one was open for 1% of the time, Pallas kernels for 11%

profile of v1, /device:TPU:1, one launch (start us, length us, event | category | flops | bytes accessed | tf_op | source)
XLA Modules:
  0.0 101.1 jit_solution(9525688152239893403)
XLA Ops:
  0.6 0.7 fusion.10
  1.4 0.8 slice.24
  2.2 4.5 %collective-permute-start = (f32[2,640]{1,0:T(2,128)S(1)}, f32[2,640]{1,0:T(2,128)S(1)}, u32[]{:S(2)}, u32[]{:S(2)}) collective-permute-start(f32[2,640]{1,0:T(2,128)S(1)} %fusion), channel_id=1, source_target_pairs={{0,4},{4,8},{8,12},{12,16},{16,20},{20,24},{24,28},{28,32},{32,36}... | collective-permute-start | bytes 15368 | tf_op jit(solution)/shard_map/ppermute | solution.py:354
  6.7 0.7 slice_select_fusion
  7.4 1.9 %collective-permute-start.1 = (f32[2,640]{1,0:T(2,128)S(1)}, f32[2,640]{1,0:T(2,128)S(1)}, u32[]{:S(2)}, u32[]{:S(2)}) collective-permute-start(f32[2,640]{1,0:T(2,128)S(1)} %pad_maximum_fusion), channel_id=1, source_target_pairs={{4,0},{8,4},{12,8},{16,12},{20,16},{24,20},{28,24},{32,28},{36,32}... | collective-permute-start | bytes 15368 | tf_op jit(solution)/shard_map/ppermute | solution.py:355
  11.3 0.0 copy-start
  11.3 0.7 copy-done
  12.0 0.0 copy-start.1
  12.0 0.7 copy-done.1
  12.7 0.0 copy-start.2
  12.7 0.7 copy-done.2
  13.4 0.0 copy-start.3
  13.4 0.7 copy-done.3
  14.1 11.5 %shard_map.103 = (bf16[2,3072,512]{2,1,0:T(8,128)(2,1)}, f32[2,3072]{1,0:T(2,128)}, f32[512,512]{1,0:T(8,128)S(1)}, f32[8,512]{1,0:T(8,128)S(1)}) custom-call(s32[1]{0:T(128)} %bitcast.refs_0_.core_ref, f32[1]{0:T(128)S(6)} %copy.25.refs_1_, f32[1]{0:T(128)S(6)} %copy.26.refs_2_, f32[1]{0:T(128)S(6)} %copy.27.refs_3_, bf16[2,3072,512]{2,1,0:T(8,128)(2,1)} %refs_6_.3, ...), custom_call_target="tpu_custom_call" | custom-call | tf_op jit(solution)/shard_map/pallas_call | solution.py:211
  25.6 0.0 collective-permute-done.refs_11_
  25.6 0.0 collective-permute-done.1.refs_12_
  25.6 7.0 %shard_map.104 = (bf16[2,3072,512]{2,1,0:T(8,128)(2,1)}, f32[2,3072]{1,0:T(2,128)}, f32[768,128]{1,0:T(8,128)S(1)}, f32[768,128]{1,0:T(8,128)S(1)}) custom-call(s32[1]{0:T(128)} %bitcast.refs_0_.core_ref, f32[1]{0:T(128)S(6)} %copy.25.refs_1_, f32[1]{0:T(128)S(6)} %copy.26.refs_2_, ...), custom_call_target="tpu_custom_call", output_to_operand_aliasing={{0}: (15, {}), {1}: (16, {})} | custom-call | tf_op jit(solution)/shard_map/pallas_call | solution.py:211
  32.5 0.0 collective-permute-start.2
  32.6 1.7 %collective-permute-done.2 = f32[768,128]{1,0:T(8,128)S(1)} collective-permute-done((f32[768,128]{1,0:T(8,128)S(1)}, f32[768,128]{1,0:T(8,128)S(1)}, u32[]{:S(2)}, u32[]{:S(2)}) %collective-permute-start.2) | collective-permute-done | bytes 393248 | tf_op jit(solution)/shard_map/ppermute | solution.py:322
  34.3 0.1 subtract_convert_fusion
  34.3 0.2 maximum_select_fusion
  34.5 22.5 %all_to_all.10 = bf16[32,24,128]{2,1,0:T(8,128)(2,1)S(1)} all-to-all(bf16[32,24,128]{2,1,0:T(8,128)(2,1)S(1)} %bitcast.23), channel_id=1, replica_groups=mesh['space_0'=8,'space_1'=4,'space_2'=2,'inst'=4] {'space_0','space_1'}, dimensions={0} | all-to-all | bytes 393216 | tf_op jit(solution)/shard_map/all_to_all | solution.py:331
  57.1 16.8 %all_to_all.11 = f32[32,24,128]{2,1,0:T(8,128)S(1)} all-to-all(f32[32,24,128]{2,1,0:T(8,128)S(1)} %broadcast_in_dim.25), channel_id=1, replica_groups=mesh['space_0'=8,'space_1'=4,'space_2'=2,'inst'=4] {'space_0','space_1'}, dimensions={0} | all-to-all | bytes 786432 | tf_op jit(solution)/shard_map/all_to_all | solution.py:333
  73.9 3.4 %collective-permute-start.3 = (f32[768,128]{1,0:T(8,128)S(1)}, f32[768,128]{1,0:T(8,128)S(1)}, u32[]{:S(2)}, u32[]{:S(2)}) collective-permute-start(f32[768,128]{1,0:T(8,128)S(1)} %bitcast.18), channel_id=1, source_target_pairs={{0,4},{4,0},{1,5},{5,1},{2,6},{6,2},{3,7},{7,3},{8,12},{12,8},{9,1... | collective-permute-start | bytes 1179656 | tf_op jit(solution)/shard_map/ppermute | solution.py:322
  77.3 1.3 %collective-permute-done.3.other_ref = f32[768,128]{1,0:T(8,128)S(1)} collective-permute-done((f32[768,128]{1,0:T(8,128)S(1)}, f32[768,128]{1,0:T(8,128)S(1)}, u32[]{:S(2)}, u32[]{:S(2)}) %collective-permute-start.3) | collective-permute-done | bytes 393248 | tf_op jit(solution)/shard_map/ppermute | solution.py:322
  78.7 22.4 %shard_map.105 = f32[1,512]{1,0:T(1,128)} custom-call(s32[1]{0:T(128)} %bitcast.refs_0_.core_ref, f32[768,128]{1,0:T(8,128)S(1)} %bitcast.19, f32[768,128]{1,0:T(8,128)S(1)} %collective-permute-done.3.other_ref), custom_call_target="tpu_custom_call" | custom-call | tf_op jit(solution)/shard_map/pallas_call | solution.py:307
  (8 shorter events, 0.1 us)
Async XLA Ops:
  2.2 23.4 %collective-permute-start = (f32[2,640]{1,0:T(2,128)S(1)}, f32[2,640]{1,0:T(2,128)S(1)}, u32[]{:S(2)}, u32[]{:S(2)}) collective-permute-start(f32[2,640]{1,0:T(2,128)S(1)} %fusion), channel_id=1, source_target_pairs={{0,4},{4,8},{8,12},{12,16},{16,20},{20,24},{24,28},{28,32},{32,36}... | collective-permute-start | bytes 15368 | tf_op jit(solution)/shard_map/ppermute | solution.py:354
  7.4 18.2 %collective-permute-start.1 = (f32[2,640]{1,0:T(2,128)S(1)}, f32[2,640]{1,0:T(2,128)S(1)}, u32[]{:S(2)}, u32[]{:S(2)}) collective-permute-start(f32[2,640]{1,0:T(2,128)S(1)} %pad_maximum_fusion), channel_id=1, source_target_pairs={{4,0},{8,4},{12,8},{16,12},{20,16},{24,20},{28,24},{32,28},{36,32}... | collective-permute-start | bytes 15368 | tf_op jit(solution)/shard_map/ppermute | solution.py:355
  11.3 0.7 copy-start
  12.0 0.7 copy-start.1
  12.7 0.7 copy-start.2
  13.4 0.7 copy-start.3
  32.5 1.7 %collective-permute-start.2 = (f32[768,128]{1,0:T(8,128)S(1)}, f32[768,128]{1,0:T(8,128)S(1)}, u32[]{:S(2)}, u32[]{:S(2)}) collective-permute-start(f32[768,128]{1,0:T(8,128)S(1)} %get-tuple-element.18), channel_id=1, source_target_pairs={{0,4},{4,0},{1,5},{5,1},{2,6},{6,2},{3,7},{7,3},{8,12},{12,8},{9,1... | collective-permute-start | bytes 1179656 | tf_op jit(solution)/shard_map/ppermute | solution.py:322
  73.9 4.8 %collective-permute-start.3 = (f32[768,128]{1,0:T(8,128)S(1)}, f32[768,128]{1,0:T(8,128)S(1)}, u32[]{:S(2)}, u32[]{:S(2)}) collective-permute-start(f32[768,128]{1,0:T(8,128)S(1)} %bitcast.18), channel_id=1, source_target_pairs={{0,4},{4,0},{1,5},{5,1},{2,6},{6,2},{3,7},{7,3},{8,12},{12,8},{9,1... | collective-permute-start | bytes 1179656 | tf_op jit(solution)/shard_map/ppermute | solution.py:322

commit v2 on v1

--- a/solution.py
+++ b/solution.py
@@ -16,7 +16,8 @@
 
 time_step = 0.5
 LANE = 128
-STEP_CELLS = 512
+STEP_CELLS = 768
+GRAM_TILES = 2
 EXACT = lax.Precision.HIGHEST
 
 
@@ -34,10 +35,10 @@
 
 def rows_kernel(*refs, steps, size, edges):
     refs = iter(refs)
-    core_ref, nu_ref, adv_ref, rate_ref, basis_ref, before_ref, after_ref = (next(refs) for _ in range(7))
+    rates_ref, basis_ref, before_ref, after_ref = (next(refs) for _ in range(4))
     ref_ref, burn_ref, now_ref, old_ref = (next(refs) for _ in range(4))
     if edges:
-        halo_low_ref, halo_high_ref, sums_ref, right_in_ref, _, _ = (next(refs) for _ in range(6))
+        core_ref, halo_low_ref, halo_high_ref, sums_ref, right_in_ref, _, _ = (next(refs) for _ in range(7))
         jac_ref, res_ref, own_ref, other_ref, acc, right, wide = refs
     else:
         jac_ref, res_ref, acc, right, wide = refs
@@ -46,7 +47,8 @@
     chunk = step * (steps - 1) if edges else step + 1
     modes = basis_ref.shape[2]
     tiles = modes // LANE
-    nu, adv, rate = nu_ref[0], adv_ref[0], rate_ref[0]
+    nu, adv, rate = (rates_ref[i : i + 1, 0:1] for i in range(3))
+    nu_row, adv_row = rates_ref[0:1, :], rates_ref[1:2, :]
     now = now_ref[...].astype(BF16)
     diff = (now_ref[...] - old_ref[...]).astype(BF16)
     now32 = now.astype(F32)
@@ -88,13 +90,26 @@
     res = [moved[0] - time_step * (flux[0] - w), moved[1] - time_step * (flux[1] + w)]
     res_ref[0:1, :] = res[0]
     res_ref[1:2, :] = res[1]
-    mid = 1.0 + time_step * (2.0 * nu + adv)
-    lower = time_step * (nu + adv)
-    upper = time_step * nu
+    mid = 1.0 + time_step * (2.0 * nu_row + adv_row)
+    lower = time_step * (nu_row + adv_row)
+    upper = time_step * nu_row
 
     def sides(k, lo):
         return lower * wide[k, 7 + lo : 7 + lo + LANE, :] + upper * wide[k, 9 + lo : 9 + lo + LANE, :]
 
+    half = modes // 2
+
+    @pl.when(first)
+    def _():
+        if edges:
+            acc[0:half, :] = sums_ref[0:half, :]
+            acc[half:, half:] = sums_ref[half:, half:]
+            right[...] = right_in_ref[...]
+        else:
+            acc[...] = jnp.zeros_like(acc)
+            right[...] = jnp.zeros_like(right)
+
+    rounded = [jnp.broadcast_to(x.astype(BF16), (8, size)) for x in res]
     for t in range(size // LANE):
         lo = LANE * t
         a_col = jnp.broadcast_to(time_step * a[:, lo : lo + LANE], (LANE, LANE)).T
@@ -109,29 +124,13 @@
             heat = heat_own * q - a_col * p - sides(tiles + m, lo)
             jac_ref[0, lo : lo + LANE, cols] = fuel.astype(BF16)
             jac_ref[1, lo : lo + LANE, cols] = heat.astype(BF16)
-    j0, j1 = jac_ref[0], jac_ref[1]
-    r = jnp.dot(jnp.broadcast_to(res[0].astype(BF16), (8, size)), j0, preferred_element_type=F32)
-    r += jnp.dot(jnp.broadcast_to(res[1].astype(BF16), (8, size)), j1, preferred_element_type=F32)
-    half = modes // 2
-    top = dot_columns(j0[:, :half], j0) + dot_columns(j1[:, :half], j1)
-    bottom = dot_columns(j0[:, half:], j0[:, half:]) + dot_columns(j1[:, half:], j1[:, half:])
-
-    @pl.when(first)
-    def _():
-        if edges:
-            acc[0:half, :] = sums_ref[0:half, :] + top
-            acc[half:, half:] = sums_ref[half:, half:] + bottom
-            right[...] = right_in_ref[...] + r
-        else:
-            acc[0:half, :] = top
-            acc[half:, half:] = bottom
-            right[...] = r
-
-    @pl.when(jnp.logical_not(first))
-    def _():
-        acc[0:half, :] += top
-        acc[half:, half:] += bottom
-        right[...] += r
+        if (t + 1) % GRAM_TILES == 0:
+            span = slice(lo + LANE - GRAM_TILES * LANE, lo + LANE)
+            j = jnp.concatenate([jac_ref[0, span, :], jac_ref[1, span, :]], axis=0)
+            both_res = jnp.concatenate([x[:, span] for x in rounded], axis=1)
+            right[...] += jnp.dot(both_res, j, preferred_element_type=F32)
+            acc[0:half, :] += dot_columns(j[:, :half], j)
+            acc[half:, half:] += dot_columns(j[:, half:], j[:, half:])
 
     if not edges:
         return
@@ -163,7 +162,7 @@
     return -(-(LANE * len(tile_pairs(count)) + 8 * count) // 512) * 512
 
 
-def rows_call(core, nu, adv, rate, basis, ref, burn, now, old, edge_args=None):
+def rows_call(rates, basis, ref, burn, now, old, edge_args=None):
     cells, modes = basis.shape[1:]
     size = STEP_CELLS
     steps = cells // size
@@ -179,7 +178,7 @@
         return pl.BlockSpec(shape, lambda i: (0,) * len(shape))
 
     in_specs = [
-        smem, smem, smem, smem,
+        whole(rates.shape),
         pl.BlockSpec((2, size, modes), lambda i: (0, chunk(i), 0)),
         pl.BlockSpec((2, 16, modes), lambda i: (0, jnp.maximum(chunk(i) * per - 1, 0), 0)),
         pl.BlockSpec((2, 16, modes), lambda i: (0, jnp.minimum(chunk(i) * per + per, cells // 16 - 1), 0)),
@@ -195,12 +194,12 @@
     ]
     sums_shape = [jax.ShapeDtypeStruct((modes, modes), F32), jax.ShapeDtypeStruct((8, modes), F32)]
     scratch = [pltpu.VMEM((2 * (modes // LANE), size + 16, LANE), F32)]
-    args = [core, nu, adv, rate, basis, basis, basis, ref, burn, now, old]
+    args = [rates, basis, basis, basis, ref, burn, now, old]
     aliases = {}
     if edges:
         anywhere = pl.BlockSpec(memory_space=pl.ANY)
         args += edge_args
-        in_specs += [whole(a.shape) for a in edge_args[:4]] + [anywhere, anywhere]
+        in_specs += [smem] + [whole(a.shape) for a in edge_args[1:5]] + [anywhere, anywhere]
         out_specs += [whole((half, LANE))] * 2
         out_shape += [jax.ShapeDtypeStruct((half, LANE), F32)] * 2
         scratch = [pltpu.VMEM(s.shape, s.dtype) for s in sums_shape] + scratch
@@ -216,14 +215,14 @@
         out_shape=out_shape,
         scratch_shapes=scratch,
         input_output_aliases=aliases,
-        compiler_params=pltpu.CompilerParams(vmem_limit_bytes=48 * 2**20),
+        compiler_params=pltpu.CompilerParams(vmem_limit_bytes=60 * 2**20),
     )(*args)
 
 
-def rows_and_sums(core, nu, adv, rate, basis, halo_low, halo_high, ref, burn, now, old):
-    common = (core, nu, adv, rate, basis, ref, burn, now, old)
+def rows_and_sums(core, rates, basis, halo_low, halo_high, ref, burn, now, old):
+    common = (rates, basis, ref, burn, now, old)
     jacobian, residual, sums, right = rows_call(*common)
-    return rows_call(*common, [halo_low, halo_high, sums, right, jacobian, residual])
+    return rows_call(*common, [core, halo_low, halo_high, sums, right, jacobian, residual])
 
 
 def reciprocal(x):
@@ -333,8 +332,41 @@
     return lax.all_to_all(copies, PLANE, 0, 0, tiled=True).reshape(shard.shape)
 
 
-def edge_message(basis_row, state_value):
-    return jnp.concatenate([basis_row.astype(F32), jnp.pad(state_value, ((0, 0), (0, LANE - 1)))], axis=1)
+def edge_kernel(
+    nu_ref, adv_ref, rate_ref, first_ref, last_ref, ref_first, ref_last, up_ref, down_ref, rates_ref
+):
+    modes = first_ref.shape[2]
+    for v in range(2):
+        up_ref[v : v + 1, :modes] = last_ref[v].astype(F32)[15:16]
+        down_ref[v : v + 1, :modes] = first_ref[v].astype(F32)[0:1]
+    up_ref[:, modes:] = jnp.broadcast_to(ref_last[:, LANE - 1 : LANE], (2, LANE))
+    down_ref[:, modes:] = jnp.broadcast_to(ref_first[:, 0:1], (2, LANE))
+    for i, scalar_ref in enumerate((nu_ref, adv_ref, rate_ref)):
+        rates_ref[i : i + 1, :] = jnp.full((1, LANE), scalar_ref[0], F32)
+
+
+def edge_messages(basis, ref, nu, adv, rate):
+    cells, modes = basis.shape[1:]
+    smem = pl.BlockSpec(memory_space=pltpu.SMEM)
+
+    def whole(shape):
+        return pl.BlockSpec(shape, lambda i: (0,) * len(shape))
+
+    shapes = [(2, modes + LANE), (2, modes + LANE), (8, LANE)]
+    return pl.pallas_call(
+        edge_kernel,
+        grid=(1,),
+        in_specs=[
+            smem, smem, smem,
+            pl.BlockSpec((2, 16, modes), lambda i: (0, 0, 0)),
+            pl.BlockSpec((2, 16, modes), lambda i: (0, cells // 16 - 1, 0)),
+            pl.BlockSpec((2, LANE), lambda i: (0, 0)),
+            pl.BlockSpec((2, LANE), lambda i: (0, cells // LANE - 1)),
+        ],
+        out_specs=[whole(shape) for shape in shapes],
+        out_shape=[jax.ShapeDtypeStruct(shape, F32) for shape in shapes],
+        compiler_params=pltpu.CompilerParams(vmem_limit_bytes=60 * 2**20),
+    )(nu, adv, rate, basis, basis, ref, ref)
 
 
 def on_device(
@@ -351,13 +383,11 @@
     size = lax.axis_size(SPACE)
     core = lax.axis_index(CORE).reshape(1)
     up = [(i, i + 1) for i in range(size - 1)]
-    halo_low = lax.ppermute(edge_message(basis_rows[:, -1], reference_state[:, -1:]), SPACE, up)
-    halo_high = lax.ppermute(
-        edge_message(basis_rows[:, 0], reference_state[:, :1]), SPACE, [(j, i) for i, j in up]
-    )
+    up_row, down_row, rates = edge_messages(basis_rows, reference_state, diffusivity, advection, reaction_rate)
+    halo_low = lax.ppermute(up_row, SPACE, up)
+    halo_high = lax.ppermute(down_row, SPACE, [(j, i) for i, j in up])
     jacobian, residual, own, other = rows_and_sums(
-        core, diffusivity, advection, reaction_rate, basis_rows, halo_low, halo_high,
-        reference_state, burning[None], coords_now, coords_before,
+        core, rates, basis_rows, halo_low, halo_high, reference_state, burning[None], coords_now, coords_before
     )
     row = core * own.shape[0] + jnp.arange(own.shape[0], dtype=jnp.int32)
     begin = LANE * len(tile_pairs(modes // LANE))

time: 102 us -> 100 us (0.980)
  local copies, waits for them, and re-layouts: 4.34 us -> 0.61 us
  other arithmetic: 1 us -> 2.3 us
    unnamed x8 -> x4, local copies, waits for them, and re-layouts: 2.8 us -> 0.58 us
    slice x2 -> x0, local copies, waits for them, and re-layouts: 1.5 us -> none  [the longest x1 0.75 us: on_device(): reference_state[:, -1:]]
    pallas_call x0 -> x1, Pallas kernels: none -> 1.46 us  [edge_messages(): pl.pallas_call(edge_kernel, grid=(1,), in_specs=[smem, smem, smem, pl.Blo...]
  transfers between devices with their start and end apart: 4 -> 4, of which waited for: 2 -> 2; matrix products, arithmetic and copies ran while one was open for 1% -> 0% of each run, Pallas kernels for 11% -> 9%
where the time goes in v2:
time: 100 us; the launch traced here: 99.8 us
  Pallas kernels  41.8 us (42%)
  blocking collectives  39.3 us (39%)
  starting transfers between devices  9.94 us (10%)
  waiting for transfers between devices  3.25 us (3%)
  between operations  2.67 us (3%)
  other arithmetic  2.3 us (2%)
    all_to_all x1, blocking collectives, summed_over_plane(): lax.all_to_all(blocks, PLANE, 0, 0, tiled=True).astype(F32)  22.5 us
    pallas_call x1, Pallas kernels, solve_update(): pl.pallas_call(functools.partial(solve_kernel, count=modes // LANE), out_...  22.4 us
    pallas_call x2, Pallas kernels, rows_call(): pl.pallas_call(functools.partial(rows_kernel, steps=steps, size=size, edg...  17.9 us
    all_to_all x1, blocking collectives, summed_over_plane(): return lax.all_to_all(copies, PLANE, 0, 0, tiled=True).reshape(shard.shape)  16.8 us
    ppermute x1, starting transfers between devices, on_device(): halo_low = lax.ppermute(up_row, SPACE, up)  4.5 us
    ppermute x2, starting transfers between devices, swapped(): return lax.ppermute(shard, CORE, [(0, 1), (1, 0)])  3.52 us
    ppermute x2, waiting for transfers between devices, swapped(): return lax.ppermute(shard, CORE, [(0, 1), (1, 0)])  3.25 us
  transfers between devices with their start and end apart: 4, of which 2 were waited for; matrix products, arithmetic and copies ran while one was open for 0% of the time, Pallas kernels for 9%

profile of v2, /device:TPU:1, one launch (start us, length us, event | category | flops | bytes accessed | tf_op | source)
XLA Modules:
  0.0 99.8 jit_solution(5029498340043075591)
XLA Ops:
  2.6 1.5 %shard_map.103 = (f32[2,640]{1,0:T(2,128)}, f32[2,640]{1,0:T(2,128)}, f32[8,128]{1,0:T(8,128)}) custom-call(f32[1]{0:T(128)S(6)} %copy.15.nu_ref, f32[1]{0:T(128)S(6)} %copy.16.adv_ref, f32[1]{0:T(128)S(6)} %copy.17.rate_ref, bf16[2,3072,512]{2,1,0:T(8,128)(2,1)} %refs_3_.3, bf16[2,3072,512]{2,1,0:T(8,128)(2,1)} %refs_3_.3, f32[2,3072]{1,0:T(2,128)} %refs_4_.3, ...), custom_call_target="tpu_custom_call" | custom-call | tf_op jit(solution)/shard_map/pallas_call | solution.py:356
  4.0 4.5 %collective-permute-start = (f32[2,640]{1,0:T(2,128)}, f32[2,640]{1,0:T(2,128)S(1)}, u32[]{:S(2)}, u32[]{:S(2)}) collective-permute-start(f32[2,640]{1,0:T(2,128)} %get-tuple-element.15), channel_id=1, source_target_pairs={{0,4},{4,8},{8,12},{12,16},{16,20},{20,24},{24,28},{28,32},{32,36}... | collective-permute-start | bytes 15368 | tf_op jit(solution)/shard_map/ppermute | solution.py:387
  8.5 1.9 %collective-permute-start.1 = (f32[2,640]{1,0:T(2,128)}, f32[2,640]{1,0:T(2,128)S(1)}, u32[]{:S(2)}, u32[]{:S(2)}) collective-permute-start(f32[2,640]{1,0:T(2,128)} %get-tuple-element.16), channel_id=1, source_target_pairs={{4,0},{8,4},{12,8},{16,12},{20,16},{24,20},{28,24},{32,28},{36,32}... | collective-permute-start | bytes 15368 | tf_op jit(solution)/shard_map/ppermute | solution.py:388
  10.5 8.8 %shard_map.104 = (bf16[2,3072,512]{2,1,0:T(8,128)(2,1)}, f32[2,3072]{1,0:T(2,128)}, f32[512,512]{1,0:T(8,128)}, f32[8,512]{1,0:T(8,128)}) custom-call(f32[8,128]{1,0:T(8,128)} %get-tuple-element.14.refs_0_, bf16[2,3072,512]{2,1,0:T(8,128)(2,1)} %refs_3_.3, bf16[2,3072,512]{2,1,0:T(8,128)(2,1)} %refs_3_.3, bf16[2,3072,512]{2,1,0:T(8,128)(2,1)} %refs_3_.3, ...), custom_call_target="tpu_custom_call" | custom-call | tf_op jit(solution)/shard_map/pallas_call | solution.py:210
  19.3 0.0 collective-permute-done.refs_9_
  19.3 0.0 copy-start
  19.3 0.0 collective-permute-done.1.refs_10_
  19.3 0.0 copy-start.1
  19.3 0.6 copy-done
  19.9 0.0 copy-done.1
  19.9 9.1 %shard_map.105 = (bf16[2,3072,512]{2,1,0:T(8,128)(2,1)}, f32[2,3072]{1,0:T(2,128)}, f32[768,128]{1,0:T(8,128)}, f32[768,128]{1,0:T(8,128)}) custom-call(f32[8,128]{1,0:T(8,128)} %get-tuple-element.14.refs_0_, bf16[2,3072,512]{2,1,0:T(8,128)(2,1)} %refs_3_.3, bf16[2,3072,512]{2,1,0:T(8,128)(2,1)} %refs_3_.3, ...), custom_call_target="tpu_custom_call", output_to_operand_aliasing={{0}: (13, {}), {1}: (14, {})} | custom-call | tf_op jit(solution)/shard_map/pallas_call | solution.py:210
  29.0 0.1 collective-permute-start.2
  29.1 1.9 %collective-permute-done.2 = f32[768,128]{1,0:T(8,128)S(1)} collective-permute-done((f32[768,128]{1,0:T(8,128)}, f32[768,128]{1,0:T(8,128)S(1)}, u32[]{:S(2)}, u32[]{:S(2)}) %collective-permute-start.2) | collective-permute-done | bytes 393248 | tf_op jit(solution)/shard_map/ppermute | solution.py:321
  31.0 1.1 %subtract_convert_fusion = bf16[768,128]{1,0:T(8,128)(2,1)S(1)} fusion(f32[768,128]{1,0:T(8,128)} %get-tuple-element.23, f32[768,128]{1,0:T(8,128)S(1)} %collective-permute-done.2), kind=kLoop, calls=%fused_computation.1 | loop fusion | flops 491520 | bytes 983040 | tf_op jit(solution)/shard_map/convert.3
  32.1 1.2 %maximum_select_fusion = bf16[768,128]{1,0:T(8,128)(2,1)S(1)} fusion(bf16[767,128]{1,0:T(8,128)(2,1)S(1)} %bitcast.12, bf16[1,128]{1,0:T(2,128)(2,1)S(1)} %slice.12, pred[768]{0:T(1024)(128)(4,1)S(1)} %fusion.6, f32[768,128]{1,0:T(8,128)} %get-tuple-element.23, f32[768,128]{1,0:T(8,128)S(1)} %collective-permute-done.2), kind=kLoop, calls=%fused_computation.2 | loop fusion | flops 688128 | bytes 1180416 | tf_op jit(solution)/shard_map/jit(_where)/select_n | solution.py:328
  33.3 22.5 %all_to_all.10 = bf16[32,24,128]{2,1,0:T(8,128)(2,1)S(1)} all-to-all(bf16[32,24,128]{2,1,0:T(8,128)(2,1)S(1)} %bitcast.11), channel_id=1, replica_groups=mesh['space_0'=8,'space_1'=4,'space_2'=2,'inst'=4] {'space_0','space_1'}, dimensions={0} | all-to-all | bytes 393216 | tf_op jit(solution)/shard_map/all_to_all | solution.py:330
  55.9 16.8 %all_to_all.11 = f32[32,24,128]{2,1,0:T(8,128)S(1)} all-to-all(f32[32,24,128]{2,1,0:T(8,128)S(1)} %broadcast_in_dim.25), channel_id=1, replica_groups=mesh['space_0'=8,'space_1'=4,'space_2'=2,'inst'=4] {'space_0','space_1'}, dimensions={0} | all-to-all | bytes 786432 | tf_op jit(solution)/shard_map/all_to_all | solution.py:332
  72.7 3.4 %collective-permute-start.3 = (f32[768,128]{1,0:T(8,128)S(1)}, f32[768,128]{1,0:T(8,128)S(1)}, u32[]{:S(2)}, u32[]{:S(2)}) collective-permute-start(f32[768,128]{1,0:T(8,128)S(1)} %bitcast.8), channel_id=1, source_target_pairs={{0,4},{4,0},{1,5},{5,1},{2,6},{6,2},{3,7},{7,3},{8,12},{12,8},{9,1... | collective-permute-start | bytes 1179656 | tf_op jit(solution)/shard_map/ppermute | solution.py:321
  76.1 1.3 %collective-permute-done.3.other_ref = f32[768,128]{1,0:T(8,128)S(1)} collective-permute-done((f32[768,128]{1,0:T(8,128)S(1)}, f32[768,128]{1,0:T(8,128)S(1)}, u32[]{:S(2)}, u32[]{:S(2)}) %collective-permute-start.3) | collective-permute-done | bytes 393248 | tf_op jit(solution)/shard_map/ppermute | solution.py:321
  77.4 22.4 %shard_map.106 = f32[1,512]{1,0:T(1,128)} custom-call(s32[1]{0:T(128)} %bitcast.1.refs_8_.core_ref, f32[768,128]{1,0:T(8,128)S(1)} %bitcast.9, f32[768,128]{1,0:T(8,128)S(1)} %collective-permute-done.3.other_ref), custom_call_target="tpu_custom_call" | custom-call | tf_op jit(solution)/shard_map/pallas_call | solution.py:306
  (4 shorter events, 0.1 us)
Async XLA Ops:
  4.0 15.2 %collective-permute-start = (f32[2,640]{1,0:T(2,128)}, f32[2,640]{1,0:T(2,128)S(1)}, u32[]{:S(2)}, u32[]{:S(2)}) collective-permute-start(f32[2,640]{1,0:T(2,128)} %get-tuple-element.15), channel_id=1, source_target_pairs={{0,4},{4,8},{8,12},{12,16},{16,20},{20,24},{24,28},{28,32},{32,36}... | collective-permute-start | bytes 15368 | tf_op jit(solution)/shard_map/ppermute | solution.py:387
  8.5 10.8 %collective-permute-start.1 = (f32[2,640]{1,0:T(2,128)}, f32[2,640]{1,0:T(2,128)S(1)}, u32[]{:S(2)}, u32[]{:S(2)}) collective-permute-start(f32[2,640]{1,0:T(2,128)} %get-tuple-element.16), channel_id=1, source_target_pairs={{4,0},{8,4},{12,8},{16,12},{20,16},{24,20},{28,24},{32,28},{36,32}... | collective-permute-start | bytes 15368 | tf_op jit(solution)/shard_map/ppermute | solution.py:388
  19.3 0.6 copy-start
  19.3 0.6 copy-start.1
  29.0 2.0 %collective-permute-start.2 = (f32[768,128]{1,0:T(8,128)}, f32[768,128]{1,0:T(8,128)S(1)}, u32[]{:S(2)}, u32[]{:S(2)}) collective-permute-start(f32[768,128]{1,0:T(8,128)} %get-tuple-element.24), channel_id=1, source_target_pairs={{0,4},{4,0},{1,5},{5,1},{2,6},{6,2},{3,7},{7,3},{8,12},{12,8},{9,1... | collective-permute-start | bytes 1179656 | tf_op jit(solution)/shard_map/ppermute | solution.py:321
  72.7 4.8 %collective-permute-start.3 = (f32[768,128]{1,0:T(8,128)S(1)}, f32[768,128]{1,0:T(8,128)S(1)}, u32[]{:S(2)}, u32[]{:S(2)}) collective-permute-start(f32[768,128]{1,0:T(8,128)S(1)} %bitcast.8), channel_id=1, source_target_pairs={{0,4},{4,0},{1,5},{5,1},{2,6},{6,2},{3,7},{7,3},{8,12},{12,8},{9,1... | collective-permute-start | bytes 1179656 | tf_op jit(solution)/shard_map/ppermute | solution.py:321

commit v3 on v2

--- a/solution.py
+++ b/solution.py
@@ -215,7 +215,7 @@
         out_shape=out_shape,
         scratch_shapes=scratch,
         input_output_aliases=aliases,
-        compiler_params=pltpu.CompilerParams(vmem_limit_bytes=60 * 2**20),
+        compiler_params=pltpu.CompilerParams(vmem_limit_bytes=(48 if edges else 60) * 2**20),
     )(*args)
 
 
@@ -239,19 +239,18 @@
         panel = groups[p]
         base = 8 * p
         cols = [jnp.broadcast_to(panel[:, base + j : base + j + 1], full) for j in range(8)]
-        entry = [[jnp.broadcast_to(cols[t][s : s + 1], full) if t >= s else None for t in range(8)] for s in range(8)]
         window = (lanes >= base) & (lanes < base + 8)
         opened = jnp.where(window, jnp.where(lanes == subs + base, 1.0, 0.0), panel)
-        rows = [jnp.broadcast_to(opened[s : s + 1], full) for s in range(8)]
-        inv = []
+        scale = jnp.zeros(full, F32)
         for j in range(8):
-            inv.append(reciprocal(entry[j][j]))
-            for s in [*range(j + 1, 8), *range(j)]:
-                mult = (entry[j][s] if s > j else entry[s][j]) * inv[j]
-                for t in range(max(s, j + 1), 8):
-                    entry[s][t] = entry[s][t] - mult * entry[j][t]
-                rows[s] = rows[s] - mult * rows[j]
-        rows = [rows[s] * inv[s] for s in range(8)]
+            inv = reciprocal(jnp.broadcast_to(cols[j][j : j + 1], full))
+            mult = jnp.where(subs == j, 0.0, cols[j]) * inv
+            scale = jnp.where(subs == j, inv, scale)
+            for t in range(j + 1, 8):
+                cols[t] = cols[t] - mult * jnp.broadcast_to(cols[t][j : j + 1], full)
+            opened = opened - mult * jnp.broadcast_to(opened[j : j + 1], full)
+        whole = opened * scale
+        rows = [jnp.broadcast_to(whole[s : s + 1], full) for s in range(8)]
         for g in range(len(groups)):
             if g == p:
                 continue
@@ -259,9 +258,6 @@
             while len(terms) > 1:
                 terms = [a + b for a, b in zip(terms[::2], terms[1::2])]
             groups[g] = jnp.where(window, 0.0, groups[g]) - terms[0]
-        whole = rows[0]
-        for s in range(1, 8):
-            whole = jnp.where(subs == s, rows[s], whole)
         groups[p] = whole
     return jnp.concatenate(groups, axis=0)
 

time: 100 us -> 96.8 us (0.968)
  Pallas kernels: 41.8 us -> 39.2 us
  other arithmetic: 2.3 us -> 0.27 us
  local copies, waits for them, and re-layouts: 0.61 us -> 2 us
    pallas_call x1, Pallas kernels: 22.4 us -> 20.3 us  [solve_update(): pl.pallas_call(functools.partial(solve_kernel, count=modes // LANE), out_...]
    unnamed x4 -> x14, local copies, waits for them, and re-layouts: 0.58 us -> 1.96 us
    another operation x1, other arithmetic: 1.07 us -> 0.05 us
    select_n x1, other arithmetic: 1.18 us -> 0.17 us  [summed_over_plane(): sent = jnp.where(low_rows, left_over, rounded)]
where the time goes in v3:
time: 96.8 us; the launch traced here: 96.4 us
  blocking collectives  39.3 us (41%)
  Pallas kernels  39.2 us (40%)
  starting transfers between devices  9.85 us (10%)
  waiting for transfers between devices  3.06 us (3%)
  between operations  2.73 us (3%)
  local copies, waits for them, and re-layouts  2 us (2%)
    all_to_all x1, blocking collectives, summed_over_plane(): lax.all_to_all(blocks, PLANE, 0, 0, tiled=True).astype(F32)  22.5 us
    pallas_call x1, Pallas kernels, solve_update(): pl.pallas_call(functools.partial(solve_kernel, count=modes // LANE), out_...  20.3 us
    pallas_call x2, Pallas kernels, rows_call(): pl.pallas_call(functools.partial(rows_kernel, steps=steps, size=size, edg...  17.5 us
    all_to_all x1, blocking collectives, summed_over_plane(): return lax.all_to_all(copies, PLANE, 0, 0, tiled=True).reshape(shard.shape)  16.8 us
    ppermute x1, starting transfers between devices, on_device(): halo_low = lax.ppermute(up_row, SPACE, up)  4.5 us
    ppermute x2, starting transfers between devices, swapped(): return lax.ppermute(shard, CORE, [(0, 1), (1, 0)])  3.43 us
    ppermute x2, waiting for transfers between devices, swapped(): return lax.ppermute(shard, CORE, [(0, 1), (1, 0)])  3.06 us
    unnamed x14, local copies, waits for them, and re-layouts  1.96 us
  transfers between devices with their start and end apart: 4, of which 2 were waited for; matrix products, arithmetic and copies ran while one was open for 0% of the time, Pallas kernels for 9%

profile of v3, /device:TPU:1, one launch (start us, length us, event | category | flops | bytes accessed | tf_op | source)
XLA Modules:
  0.0 96.4 jit_solution(4396213379000003896)
XLA Ops:
  2.6 1.5 %shard_map.103 = (f32[2,640]{1,0:T(2,128)}, f32[2,640]{1,0:T(2,128)}, f32[8,128]{1,0:T(8,128)}) custom-call(f32[1]{0:T(128)S(6)} %copy.15.nu_ref, f32[1]{0:T(128)S(6)} %copy.16.adv_ref, f32[1]{0:T(128)S(6)} %copy.17.rate_ref, bf16[2,3072,512]{2,1,0:T(8,128)(2,1)} %refs_3_.3, bf16[2,3072,512]{2,1,0:T(8,128)(2,1)} %refs_3_.3, f32[2,3072]{1,0:T(2,128)} %refs_4_.3, ...), custom_call_target="tpu_custom_call" | custom-call | tf_op jit(solution)/shard_map/pallas_call | solution.py:352
  4.0 4.5 %collective-permute-start = (f32[2,640]{1,0:T(2,128)}, f32[2,640]{1,0:T(2,128)S(1)}, u32[]{:S(2)}, u32[]{:S(2)}) collective-permute-start(f32[2,640]{1,0:T(2,128)} %get-tuple-element.15), channel_id=1, source_target_pairs={{0,4},{4,8},{8,12},{12,16},{16,20},{20,24},{24,28},{28,32},{32,36}... | collective-permute-start | bytes 15368 | tf_op jit(solution)/shard_map/ppermute | solution.py:383
  8.5 1.9 %collective-permute-start.1 = (f32[2,640]{1,0:T(2,128)}, f32[2,640]{1,0:T(2,128)S(1)}, u32[]{:S(2)}, u32[]{:S(2)}) collective-permute-start(f32[2,640]{1,0:T(2,128)} %get-tuple-element.16), channel_id=1, source_target_pairs={{4,0},{8,4},{12,8},{16,12},{20,16},{24,20},{28,24},{32,28},{36,32}... | collective-permute-start | bytes 15368 | tf_op jit(solution)/shard_map/ppermute | solution.py:384
  10.5 0.0 copy-start.1
  10.5 0.0 copy-start.2
  10.5 0.0 copy-start.4
  10.5 0.0 copy-start.5
  10.5 0.0 copy-start.6
  10.5 9.0 %shard_map.104 = (bf16[2,3072,512]{2,1,0:T(8,128)(2,1)}, f32[2,3072]{1,0:T(2,128)}, f32[512,512]{1,0:T(8,128)}, f32[8,512]{1,0:T(8,128)}) custom-call(f32[8,128]{1,0:T(8,128)} %get-tuple-element.14.refs_0_, bf16[2,3072,512]{2,1,0:T(8,128)(2,1)} %refs_3_.3, bf16[2,3072,512]{2,1,0:T(8,128)(2,1)} %refs_3_.3, bf16[2,3072,512]{2,1,0:T(8,128)(2,1)} %refs_3_.3, ...), custom_call_target="tpu_custom_call" | custom-call | tf_op jit(solution)/shard_map/pallas_call | solution.py:210
  19.6 0.0 collective-permute-done.refs_9_
  19.6 0.0 collective-permute-done.1.refs_10_
  19.6 0.0 copy-done.1
  19.6 0.0 copy-done.2
  19.6 0.0 copy-done.4
  19.6 0.0 copy-done.5
  19.6 0.0 copy-done.6
  19.6 0.0 copy-start
  19.7 1.2 %copy-done = f32[512,512]{1,0:T(8,128)S(1)} copy-done((f32[512,512]{1,0:T(8,128)S(1)}, f32[512,512]{1,0:T(8,128)}, u32[]{:S(2)}) %copy-start) | copy-done | bytes 1048600
  20.9 0.0 copy-start.3
  20.9 0.7 copy-done.3
  21.6 8.4 %shard_map.105 = (bf16[2,3072,512]{2,1,0:T(8,128)(2,1)}, f32[2,3072]{1,0:T(2,128)}, f32[768,128]{1,0:T(8,128)S(1)}, f32[768,128]{1,0:T(8,128)S(1)}) custom-call(f32[8,128]{1,0:T(8,128)S(1)} %copy-done.4, bf16[2,3072,512]{2,1,0:T(8,128)(2,1)} %refs_3_.3, bf16[2,3072,512]{2,1,0:T(8,128)(2,1)} %refs_3_.3, ...), custom_call_target="tpu_custom_call", output_to_operand_aliasing={{0}: (13, {}), {1}: (14, {})} | custom-call | tf_op jit(solution)/shard_map/pallas_call | solution.py:210
  30.0 0.0 collective-permute-start.2
  30.0 1.7 %collective-permute-done.2 = f32[768,128]{1,0:T(8,128)S(1)} collective-permute-done((f32[768,128]{1,0:T(8,128)S(1)}, f32[768,128]{1,0:T(8,128)S(1)}, u32[]{:S(2)}, u32[]{:S(2)}) %collective-permute-start.2) | collective-permute-done | bytes 393248 | tf_op jit(solution)/shard_map/ppermute | solution.py:317
  31.8 0.2 maximum_select_fusion
  32.0 22.5 %all_to_all.10 = bf16[32,24,128]{2,1,0:T(8,128)(2,1)S(1)} all-to-all(bf16[32,24,128]{2,1,0:T(8,128)(2,1)S(1)} %bitcast.13), channel_id=1, replica_groups=mesh['space_0'=8,'space_1'=4,'space_2'=2,'inst'=4] {'space_0','space_1'}, dimensions={0} | all-to-all | bytes 393216 | tf_op jit(solution)/shard_map/all_to_all | solution.py:326
  54.6 16.8 %all_to_all.11 = f32[32,24,128]{2,1,0:T(8,128)S(1)} all-to-all(f32[32,24,128]{2,1,0:T(8,128)S(1)} %broadcast_in_dim.25), channel_id=1, replica_groups=mesh['space_0'=8,'space_1'=4,'space_2'=2,'inst'=4] {'space_0','space_1'}, dimensions={0} | all-to-all | bytes 786432 | tf_op jit(solution)/shard_map/all_to_all | solution.py:328
  71.3 3.4 %collective-permute-start.3 = (f32[768,128]{1,0:T(8,128)S(1)}, f32[768,128]{1,0:T(8,128)S(1)}, u32[]{:S(2)}, u32[]{:S(2)}) collective-permute-start(f32[768,128]{1,0:T(8,128)S(1)} %bitcast.8), channel_id=1, source_target_pairs={{0,4},{4,0},{1,5},{5,1},{2,6},{6,2},{3,7},{7,3},{8,12},{12,8},{9,1... | collective-permute-start | bytes 1179656 | tf_op jit(solution)/shard_map/ppermute | solution.py:317
  74.8 1.3 %collective-permute-done.3.other_ref = f32[768,128]{1,0:T(8,128)S(1)} collective-permute-done((f32[768,128]{1,0:T(8,128)S(1)}, f32[768,128]{1,0:T(8,128)S(1)}, u32[]{:S(2)}, u32[]{:S(2)}) %collective-permute-start.3) | collective-permute-done | bytes 393248 | tf_op jit(solution)/shard_map/ppermute | solution.py:317
  76.1 20.3 %shard_map.106 = f32[1,512]{1,0:T(1,128)} custom-call(s32[1]{0:T(128)} %bitcast.1.refs_8_.core_ref, f32[768,128]{1,0:T(8,128)S(1)} %bitcast.9, f32[768,128]{1,0:T(8,128)S(1)} %collective-permute-done.3.other_ref), custom_call_target="tpu_custom_call" | custom-call | tf_op jit(solution)/shard_map/pallas_call | solution.py:302
  (5 shorter events, 0.1 us)
Async XLA Ops:
  4.0 15.6 %collective-permute-start = (f32[2,640]{1,0:T(2,128)}, f32[2,640]{1,0:T(2,128)S(1)}, u32[]{:S(2)}, u32[]{:S(2)}) collective-permute-start(f32[2,640]{1,0:T(2,128)} %get-tuple-element.15), channel_id=1, source_target_pairs={{0,4},{4,8},{8,12},{12,16},{16,20},{20,24},{24,28},{28,32},{32,36}... | collective-permute-start | bytes 15368 | tf_op jit(solution)/shard_map/ppermute | solution.py:383
  8.5 11.1 %collective-permute-start.1 = (f32[2,640]{1,0:T(2,128)}, f32[2,640]{1,0:T(2,128)S(1)}, u32[]{:S(2)}, u32[]{:S(2)}) collective-permute-start(f32[2,640]{1,0:T(2,128)} %get-tuple-element.16), channel_id=1, source_target_pairs={{4,0},{8,4},{12,8},{16,12},{20,16},{24,20},{28,24},{32,28},{36,32}... | collective-permute-start | bytes 15368 | tf_op jit(solution)/shard_map/ppermute | solution.py:384
  10.5 9.1 %copy-start.1 = (f32[2,3072]{1,0:T(2,128)S(1)}, f32[2,3072]{1,0:T(2,128)}, u32[]{:S(2)}) copy-start(f32[2,3072]{1,0:T(2,128)} %refs_4_.3) | copy-start | bytes 73732
  10.5 9.1 %copy-start.2 = (s32[3072]{0:T(1024)S(1)}, s32[3072]{0:T(1024)}, u32[]{:S(2)}) copy-start(s32[3072]{0:T(1024)} %param.10) | copy-start | bytes 36868
  10.5 9.1 %copy-start.4 = (f32[8,128]{1,0:T(8,128)S(1)}, f32[8,128]{1,0:T(8,128)}, u32[]{:S(2)}) copy-start(f32[8,128]{1,0:T(8,128)} %get-tuple-element.14.refs_0_) | copy-start | bytes 12292
  10.5 9.1 %copy-start.5 = (f32[1,512]{1,0:T(1,128)S(1)}, f32[1,512]{1,0:T(1,128)}, u32[]{:S(2)}) copy-start(f32[1,512]{1,0:T(1,128)} %refs_6_.3) | copy-start | bytes 6148
  10.5 9.1 %copy-start.6 = (f32[1,512]{1,0:T(1,128)S(1)}, f32[1,512]{1,0:T(1,128)}, u32[]{:S(2)}) copy-start(f32[1,512]{1,0:T(1,128)} %refs_7_.3) | copy-start | bytes 6148
  19.6 1.2 %copy-start = (f32[512,512]{1,0:T(8,128)S(1)}, f32[512,512]{1,0:T(8,128)}, u32[]{:S(2)}) copy-start(f32[512,512]{1,0:T(8,128)} %get-tuple-element.17.refs_11_) | copy-start | bytes 3145732
  20.9 0.7 copy-start.3
  30.0 1.7 %collective-permute-start.2 = (f32[768,128]{1,0:T(8,128)S(1)}, f32[768,128]{1,0:T(8,128)S(1)}, u32[]{:S(2)}, u32[]{:S(2)}) collective-permute-start(f32[768,128]{1,0:T(8,128)S(1)} %get-tuple-element.24), channel_id=1, source_target_pairs={{0,4},{4,0},{1,5},{5,1},{2,6},{6,2},{3,7},{7,3},{8,12},{12,8},{9,1... | collective-permute-start | bytes 1179656 | tf_op jit(solution)/shard_map/ppermute | solution.py:317
  71.3 4.8 %collective-permute-start.3 = (f32[768,128]{1,0:T(8,128)S(1)}, f32[768,128]{1,0:T(8,128)S(1)}, u32[]{:S(2)}, u32[]{:S(2)}) collective-permute-start(f32[768,128]{1,0:T(8,128)S(1)} %bitcast.8), channel_id=1, source_target_pairs={{0,4},{4,0},{1,5},{5,1},{2,6},{6,2},{3,7},{7,3},{8,12},{12,8},{9,1... | collective-permute-start | bytes 1179656 | tf_op jit(solution)/shard_map/ppermute | solution.py:317

commit v4 on v3

--- a/solution.py
+++ b/solution.py
@@ -38,10 +38,10 @@
     rates_ref, basis_ref, before_ref, after_ref = (next(refs) for _ in range(4))
     ref_ref, burn_ref, now_ref, old_ref = (next(refs) for _ in range(4))
     if edges:
-        core_ref, halo_low_ref, halo_high_ref, sums_ref, right_in_ref, _, _ = (next(refs) for _ in range(7))
-        jac_ref, res_ref, own_ref, other_ref, acc, right, wide = refs
+        core_ref, halo_low_ref, halo_high_ref, sums_ref, _, _ = (next(refs) for _ in range(6))
+        jac_ref, res_ref, own_ref, other_ref, acc, wide = refs
     else:
-        jac_ref, res_ref, acc, right, wide = refs
+        jac_ref, res_ref, acc, wide = refs
     step = pl.program_id(0)
     first, last = step == 0, step == pl.num_programs(0) - 1
     chunk = step * (steps - 1) if edges else step + 1
@@ -104,10 +104,9 @@
         if edges:
             acc[0:half, :] = sums_ref[0:half, :]
             acc[half:, half:] = sums_ref[half:, half:]
-            right[...] = right_in_ref[...]
+            acc[modes:, :half] = sums_ref[modes:, :half]
         else:
             acc[...] = jnp.zeros_like(acc)
-            right[...] = jnp.zeros_like(right)
 
     rounded = [jnp.broadcast_to(x.astype(BF16), (8, size)) for x in res]
     for t in range(size // LANE):
@@ -128,9 +127,9 @@
             span = slice(lo + LANE - GRAM_TILES * LANE, lo + LANE)
             j = jnp.concatenate([jac_ref[0, span, :], jac_ref[1, span, :]], axis=0)
             both_res = jnp.concatenate([x[:, span] for x in rounded], axis=1)
-            right[...] += jnp.dot(both_res, j, preferred_element_type=F32)
+            acc[modes:, :] += jnp.dot(both_res, j, preferred_element_type=F32)
             acc[0:half, :] += dot_columns(j[:, :half], j)
-            acc[half:, half:] += dot_columns(j[:, half:], j[:, half:])
+            acc[half:modes, half:] += dot_columns(j[:, half:], j[:, half:])
 
     if not edges:
         return
@@ -147,7 +146,7 @@
         if 0 <= at < rows_half:
             target[at:, :] = jnp.zeros((rows_half - at, LANE), F32)
             for i in range(modes // LANE):
-                target[at + 8 * i : at + 8 * i + 1, :] = right[0:1, LANE * i : LANE * i + LANE]
+                target[at + 8 * i : at + 8 * i + 1, :] = acc[modes : modes + 1, LANE * i : LANE * i + LANE]
 
     for core in range(2):
 
@@ -192,14 +191,14 @@
         jax.ShapeDtypeStruct((2, cells, modes), BF16),
         jax.ShapeDtypeStruct((2, cells), F32),
     ]
-    sums_shape = [jax.ShapeDtypeStruct((modes, modes), F32), jax.ShapeDtypeStruct((8, modes), F32)]
+    sums_shape = [jax.ShapeDtypeStruct((modes + 8, modes), F32)]
     scratch = [pltpu.VMEM((2 * (modes // LANE), size + 16, LANE), F32)]
     args = [rates, basis, basis, basis, ref, burn, now, old]
     aliases = {}
     if edges:
         anywhere = pl.BlockSpec(memory_space=pl.ANY)
         args += edge_args
-        in_specs += [smem] + [whole(a.shape) for a in edge_args[1:5]] + [anywhere, anywhere]
+        in_specs += [smem] + [whole(a.shape) for a in edge_args[1:4]] + [anywhere, anywhere]
         out_specs += [whole((half, LANE))] * 2
         out_shape += [jax.ShapeDtypeStruct((half, LANE), F32)] * 2
         scratch = [pltpu.VMEM(s.shape, s.dtype) for s in sums_shape] + scratch
@@ -221,8 +220,8 @@
 
 def rows_and_sums(core, rates, basis, halo_low, halo_high, ref, burn, now, old):
     common = (rates, basis, ref, burn, now, old)
-    jacobian, residual, sums, right = rows_call(*common)
-    return rows_call(*common, [core, halo_low, halo_high, sums, right, jacobian, residual])
+    jacobian, residual, sums = rows_call(*common)
+    return rows_call(*common, [core, halo_low, halo_high, sums, jacobian, residual])
 
 
 def reciprocal(x):
@@ -251,9 +250,8 @@
             opened = opened - mult * jnp.broadcast_to(opened[j : j + 1], full)
         whole = opened * scale
         rows = [jnp.broadcast_to(whole[s : s + 1], full) for s in range(8)]
-        for g in range(len(groups)):
-            if g == p:
-                continue
+        order = [*range(p + 1, len(groups)), *range(p)]
+        for g in order:
             terms = [jnp.broadcast_to(groups[g][:, base + s : base + s + 1], full) * rows[s] for s in range(8)]
             while len(terms) > 1:
                 terms = [a + b for a, b in zip(terms[::2], terms[1::2])]

time: 96.8 us -> 95.7 us (0.989)
    unnamed x14 -> x12, local copies, waits for them, and re-layouts: 1.96 us -> 1.25 us
where the time goes in v4:
time: 95.7 us; the launch traced here: 95.3 us
  blocking collectives  39.3 us (41%)
  Pallas kernels  38.8 us (41%)
  starting transfers between devices  9.85 us (10%)
  waiting for transfers between devices  3.06 us (3%)
  between operations  2.72 us (3%)
  local copies, waits for them, and re-layouts  1.29 us (1%)
    all_to_all x1, blocking collectives, summed_over_plane(): lax.all_to_all(blocks, PLANE, 0, 0, tiled=True).astype(F32)  22.5 us
    pallas_call x1, Pallas kernels, solve_update(): pl.pallas_call(functools.partial(solve_kernel, count=modes // LANE), out_...  19.9 us
    pallas_call x2, Pallas kernels, rows_call(): pl.pallas_call(functools.partial(rows_kernel, steps=steps, size=size, edg...  17.5 us
    all_to_all x1, blocking collectives, summed_over_plane(): return lax.all_to_all(copies, PLANE, 0, 0, tiled=True).reshape(shard.shape)  16.8 us
    ppermute x1, starting transfers between devices, on_device(): halo_low = lax.ppermute(up_row, SPACE, up)  4.5 us
    ppermute x2, starting transfers between devices, swapped(): return lax.ppermute(shard, CORE, [(0, 1), (1, 0)])  3.43 us
    ppermute x2, waiting for transfers between devices, swapped(): return lax.ppermute(shard, CORE, [(0, 1), (1, 0)])  3.06 us
    ppermute x1, starting transfers between devices, on_device(): halo_high = lax.ppermute(down_row, SPACE, [(j, i) for i, j in up])  1.93 us
  transfers between devices with their start and end apart: 4, of which 2 were waited for; matrix products, arithmetic and copies ran while one was open for 0% of the time, Pallas kernels for 9%

profile of v4, /device:TPU:1, one launch (start us, length us, event | category | flops | bytes accessed | tf_op | source)
XLA Modules:
  0.0 95.3 jit_solution(11104679058443894948)
XLA Ops:
  2.6 1.5 %shard_map.103 = (f32[2,640]{1,0:T(2,128)}, f32[2,640]{1,0:T(2,128)}, f32[8,128]{1,0:T(8,128)}) custom-call(f32[1]{0:T(128)S(6)} %copy.15.nu_ref, f32[1]{0:T(128)S(6)} %copy.16.adv_ref, f32[1]{0:T(128)S(6)} %copy.17.rate_ref, bf16[2,3072,512]{2,1,0:T(8,128)(2,1)} %refs_3_.3, bf16[2,3072,512]{2,1,0:T(8,128)(2,1)} %refs_3_.3, f32[2,3072]{1,0:T(2,128)} %refs_4_.3, ...), custom_call_target="tpu_custom_call" | custom-call | tf_op jit(solution)/shard_map/pallas_call | solution.py:350
  4.0 4.5 %collective-permute-start = (f32[2,640]{1,0:T(2,128)}, f32[2,640]{1,0:T(2,128)S(1)}, u32[]{:S(2)}, u32[]{:S(2)}) collective-permute-start(f32[2,640]{1,0:T(2,128)} %get-tuple-element.14), channel_id=1, source_target_pairs={{0,4},{4,8},{8,12},{12,16},{16,20},{20,24},{24,28},{28,32},{32,36}... | collective-permute-start | bytes 15368 | tf_op jit(solution)/shard_map/ppermute | solution.py:381
  8.5 1.9 %collective-permute-start.1 = (f32[2,640]{1,0:T(2,128)}, f32[2,640]{1,0:T(2,128)S(1)}, u32[]{:S(2)}, u32[]{:S(2)}) collective-permute-start(f32[2,640]{1,0:T(2,128)} %get-tuple-element.15), channel_id=1, source_target_pairs={{4,0},{8,4},{12,8},{16,12},{20,16},{24,20},{28,24},{32,28},{36,32}... | collective-permute-start | bytes 15368 | tf_op jit(solution)/shard_map/ppermute | solution.py:382
  10.5 0.0 copy-start.1
  10.5 0.0 copy-start.2
  10.5 0.0 copy-start.3
  10.5 0.0 copy-start.4
  10.5 0.0 copy-start.5
  10.5 9.0 %shard_map.104 = (bf16[2,3072,512]{2,1,0:T(8,128)(2,1)}, f32[2,3072]{1,0:T(2,128)}, f32[520,512]{1,0:T(8,128)}) custom-call(f32[8,128]{1,0:T(8,128)} %get-tuple-element.13.refs_0_, bf16[2,3072,512]{2,1,0:T(8,128)(2,1)} %refs_3_.3, bf16[2,3072,512]{2,1,0:T(8,128)(2,1)} %refs_3_.3, bf16[2,3072,512]{2,1,0:T(8,128)(2,1)} %refs_3_.3, f32[2,3072]{1,0:T(2,128)} %refs_4_.3, ...), custom_call_target="tpu_custom_call" | custom-call | tf_op jit(solution)/shard_map/pallas_call | solution.py:209
  19.6 0.0 collective-permute-done.refs_9_
  19.6 0.0 collective-permute-done.1.refs_10_
  19.6 0.0 copy-done.1
  19.6 0.0 copy-done.2
  19.6 0.0 copy-done.3
  19.6 0.0 copy-done.4
  19.6 0.0 copy-done.5
  19.7 0.0 copy-start
  19.7 1.2 %copy-done = f32[520,512]{1,0:T(8,128)S(1)} copy-done((f32[520,512]{1,0:T(8,128)S(1)}, f32[520,512]{1,0:T(8,128)}, u32[]{:S(2)}) %copy-start) | copy-done | bytes 1064984
  20.9 8.4 %shard_map.105 = (bf16[2,3072,512]{2,1,0:T(8,128)(2,1)}, f32[2,3072]{1,0:T(2,128)}, f32[768,128]{1,0:T(8,128)S(1)}, f32[768,128]{1,0:T(8,128)S(1)}) custom-call(f32[8,128]{1,0:T(8,128)S(1)} %copy-done.3, bf16[2,3072,512]{2,1,0:T(8,128)(2,1)} %refs_3_.3, bf16[2,3072,512]{2,1,0:T(8,128)(2,1)} %refs_3_.3, ...), custom_call_target="tpu_custom_call", output_to_operand_aliasing={{0}: (12, {}), {1}: (13, {})} | custom-call | tf_op jit(solution)/shard_map/pallas_call | solution.py:209
  29.3 0.0 collective-permute-start.2
  29.3 1.7 %collective-permute-done.2 = f32[768,128]{1,0:T(8,128)S(1)} collective-permute-done((f32[768,128]{1,0:T(8,128)S(1)}, f32[768,128]{1,0:T(8,128)S(1)}, u32[]{:S(2)}, u32[]{:S(2)}) %collective-permute-start.2) | collective-permute-done | bytes 393248 | tf_op jit(solution)/shard_map/ppermute | solution.py:315
  31.1 0.2 maximum_select_fusion
  31.3 22.5 %all_to_all.10 = bf16[32,24,128]{2,1,0:T(8,128)(2,1)S(1)} all-to-all(bf16[32,24,128]{2,1,0:T(8,128)(2,1)S(1)} %bitcast.13), channel_id=1, replica_groups=mesh['space_0'=8,'space_1'=4,'space_2'=2,'inst'=4] {'space_0','space_1'}, dimensions={0} | all-to-all | bytes 393216 | tf_op jit(solution)/shard_map/all_to_all | solution.py:324
  53.9 16.8 %all_to_all.11 = f32[32,24,128]{2,1,0:T(8,128)S(1)} all-to-all(f32[32,24,128]{2,1,0:T(8,128)S(1)} %broadcast_in_dim.25), channel_id=1, replica_groups=mesh['space_0'=8,'space_1'=4,'space_2'=2,'inst'=4] {'space_0','space_1'}, dimensions={0} | all-to-all | bytes 786432 | tf_op jit(solution)/shard_map/all_to_all | solution.py:326
  70.6 3.4 %collective-permute-start.3 = (f32[768,128]{1,0:T(8,128)S(1)}, f32[768,128]{1,0:T(8,128)S(1)}, u32[]{:S(2)}, u32[]{:S(2)}) collective-permute-start(f32[768,128]{1,0:T(8,128)S(1)} %bitcast.8), channel_id=1, source_target_pairs={{0,4},{4,0},{1,5},{5,1},{2,6},{6,2},{3,7},{7,3},{8,12},{12,8},{9,1... | collective-permute-start | bytes 1179656 | tf_op jit(solution)/shard_map/ppermute | solution.py:315
  74.1 1.3 %collective-permute-done.3.other_ref = f32[768,128]{1,0:T(8,128)S(1)} collective-permute-done((f32[768,128]{1,0:T(8,128)S(1)}, f32[768,128]{1,0:T(8,128)S(1)}, u32[]{:S(2)}, u32[]{:S(2)}) %collective-permute-start.3) | collective-permute-done | bytes 393248 | tf_op jit(solution)/shard_map/ppermute | solution.py:315
  75.4 19.9 %shard_map.106 = f32[1,512]{1,0:T(1,128)} custom-call(s32[1]{0:T(128)} %bitcast.1.refs_8_.core_ref, f32[768,128]{1,0:T(8,128)S(1)} %bitcast.9, f32[768,128]{1,0:T(8,128)S(1)} %collective-permute-done.3.other_ref), custom_call_target="tpu_custom_call" | custom-call | tf_op jit(solution)/shard_map/pallas_call | solution.py:300
  (5 shorter events, 0.1 us)
Async XLA Ops:
  4.0 15.6 %collective-permute-start = (f32[2,640]{1,0:T(2,128)}, f32[2,640]{1,0:T(2,128)S(1)}, u32[]{:S(2)}, u32[]{:S(2)}) collective-permute-start(f32[2,640]{1,0:T(2,128)} %get-tuple-element.14), channel_id=1, source_target_pairs={{0,4},{4,8},{8,12},{12,16},{16,20},{20,24},{24,28},{28,32},{32,36}... | collective-permute-start | bytes 15368 | tf_op jit(solution)/shard_map/ppermute | solution.py:381
  8.5 11.1 %collective-permute-start.1 = (f32[2,640]{1,0:T(2,128)}, f32[2,640]{1,0:T(2,128)S(1)}, u32[]{:S(2)}, u32[]{:S(2)}) collective-permute-start(f32[2,640]{1,0:T(2,128)} %get-tuple-element.15), channel_id=1, source_target_pairs={{4,0},{8,4},{12,8},{16,12},{20,16},{24,20},{28,24},{32,28},{36,32}... | collective-permute-start | bytes 15368 | tf_op jit(solution)/shard_map/ppermute | solution.py:382
  10.5 9.1 %copy-start.1 = (f32[2,3072]{1,0:T(2,128)S(1)}, f32[2,3072]{1,0:T(2,128)}, u32[]{:S(2)}) copy-start(f32[2,3072]{1,0:T(2,128)} %refs_4_.3) | copy-start | bytes 73732
  10.5 9.1 %copy-start.2 = (s32[3072]{0:T(1024)S(1)}, s32[3072]{0:T(1024)}, u32[]{:S(2)}) copy-start(s32[3072]{0:T(1024)} %param.10) | copy-start | bytes 36868
  10.5 9.1 %copy-start.3 = (f32[8,128]{1,0:T(8,128)S(1)}, f32[8,128]{1,0:T(8,128)}, u32[]{:S(2)}) copy-start(f32[8,128]{1,0:T(8,128)} %get-tuple-element.13.refs_0_) | copy-start | bytes 12292
  10.5 9.1 %copy-start.4 = (f32[1,512]{1,0:T(1,128)S(1)}, f32[1,512]{1,0:T(1,128)}, u32[]{:S(2)}) copy-start(f32[1,512]{1,0:T(1,128)} %refs_6_.3) | copy-start | bytes 6148
  10.5 9.1 %copy-start.5 = (f32[1,512]{1,0:T(1,128)S(1)}, f32[1,512]{1,0:T(1,128)}, u32[]{:S(2)}) copy-start(f32[1,512]{1,0:T(1,128)} %refs_7_.3) | copy-start | bytes 6148
  19.7 1.2 %copy-start = (f32[520,512]{1,0:T(8,128)S(1)}, f32[520,512]{1,0:T(8,128)}, u32[]{:S(2)}) copy-start(f32[520,512]{1,0:T(8,128)} %get-tuple-element.16.refs_11_) | copy-start | bytes 3194884
  29.3 1.7 %collective-permute-start.2 = (f32[768,128]{1,0:T(8,128)S(1)}, f32[768,128]{1,0:T(8,128)S(1)}, u32[]{:S(2)}, u32[]{:S(2)}) collective-permute-start(f32[768,128]{1,0:T(8,128)S(1)} %get-tuple-element.22), channel_id=1, source_target_pairs={{0,4},{4,0},{1,5},{5,1},{2,6},{6,2},{3,7},{7,3},{8,12},{12,8},{9,1... | collective-permute-start | bytes 1179656 | tf_op jit(solution)/shard_map/ppermute | solution.py:315
  70.6 4.8 %collective-permute-start.3 = (f32[768,128]{1,0:T(8,128)S(1)}, f32[768,128]{1,0:T(8,128)S(1)}, u32[]{:S(2)}, u32[]{:S(2)}) collective-permute-start(f32[768,128]{1,0:T(8,128)S(1)} %bitcast.8), channel_id=1, source_target_pairs={{0,4},{4,0},{1,5},{5,1},{2,6},{6,2},{3,7},{7,3},{8,12},{12,8},{9,1... | collective-permute-start | bytes 1179656 | tf_op jit(solution)/shard_map/ppermute | solution.py:315
